TPU v7x, 32 devices: a whole 2x2x4 slice. The times are simulated.
32 devices in a mesh: models: 2 (over y), gx: 8 (over z, x), gz: 2 (over core).
Axes of the slice: x: 2, y: 2, z: 4, core: 2. Of those that a mesh axis runs over, the one named last changes fastest.
Arguments:
- phases: int32 [32, 128, 512], P(('models', 'gz'), 'gx'), parts along dimension 0, may hold values from 0 to 7
- velocity: float32 [3, 32, 128, 512], P(None, ('models', 'gz'), 'gx'), parts along dimension 1, may hold values from -6 to 6
- pressure: float32 [32, 128, 512], P(('models', 'gz'), 'gx'), parts along dimension 0, may hold values from -6 to 6
- density_table: float32 [8], replicated, may hold values from -4.5 to 4.5
- viscosity_table: float32 [8], replicated, may hold values from 0.5 to 8
Outputs:
- velocity_out: float32 [3, 32, 128, 512], P(None, ('models', 'gz'), 'gx'), parts along dimension 1
- pressure_out: float32 [32, 128, 512], P(('models', 'gz'), 'gx'), parts along dimension 0
- gravity: float32 [256, 512], P(('models', 'gx')), parts along dimension 0
There are 2 independent parts, one for each index of `models`. A program takes and returns all parts, laid end to end along the dimension named above; an argument that names none is the same for every part. Nothing has to cross between parts.
All inputs are finite; a program needn't handle non-finite values.
Results may differ from a plain program's by a relative error of at most 0.00015.
Values sent between devices are 32-bit elements; how exact they have to be, the bound alone decides.
A program may use at most 64 MiB of HBM per device.

v0:
```python
import functools
import math

import jax
import jax.numpy as jnp
import numpy as np
from jax import lax
from jax.experimental import pallas as pl
from jax.experimental.pallas import tpu as pltpu
from jax.sharding import PartitionSpec as P

NY = 512
ITERS = 2


velocity_rate = 0.1
pressure_rate = 0.5
bulk_time = 2.0
shear_time = 4.0
squeeze = 0.25
gravity_scale = 4.0
layer_depth = 0.125
highest = lax.Precision.HIGHEST


def with_halo(block, sides, width):
    for axis, dim in sides:
        count = lax.axis_size(axis)
        forward = [(i, i + 1) for i in range(count - 1)]
        backward = [(target, source) for source, target in forward]
        low = lax.ppermute(
            lax.slice_in_dim(block, block.shape[dim] - width, None, axis=dim), axis, forward
        )
        high = lax.ppermute(lax.slice_in_dim(block, 0, width, axis=dim), axis, backward)
        block = jnp.concatenate([low, block, high], axis=dim)
    return block


def neighbour(field, dim_index, offset):
    lead_count = field.ndim - 3
    pieces = [slice(None)] * lead_count + [slice(1, -1), slice(1, -1), slice(1, -1)]
    pieces[lead_count + dim_index] = slice(2, None) if offset > 0 else slice(0, -2)
    return field[tuple(pieces)]


def center(field):
    lead_count = field.ndim - 3
    pieces = [slice(None)] * lead_count + [slice(1, -1), slice(1, -1), slice(1, -1)]
    return field[tuple(pieces)]


def relaxation(fields, viscous, density, previous):
    padded = jnp.pad(fields, ((0, 0), (0, 0), (0, 0), (1, 1)))
    eta_full = jnp.pad(viscous, ((0, 0), (0, 0), (1, 1)))
    eta_core = center(eta_full)
    pressure_full = padded[3]
    results = []
    for component, dim_index in ((0, 1), (1, 2), (2, 0)):
        moving = padded[component]
        moving_core = center(moving)
        stress = jnp.zeros_like(moving_core)
        for facing in range(3):
            for offset in (1, -1):
                face_eta = 0.5 * (eta_core + neighbour(eta_full, facing, offset))
                stress = stress + face_eta * (neighbour(moving, facing, offset) - moving_core)
        forcing = stress - 0.5 * (
            neighbour(pressure_full, dim_index, 1) - neighbour(pressure_full, dim_index, -1)
        )
        if component == 2:
            forcing = forcing - density[1:-1, 1:-1, :]
        results.append(moving_core + velocity_rate * forcing / eta_core)
    spread = jnp.zeros_like(eta_core)
    for component, dim_index in ((0, 1), (1, 2), (2, 0)):
        spread = spread + 0.5 * (
            neighbour(padded[component], dim_index, 1) - neighbour(padded[component], dim_index, -1)
        )
    pressure_core = center(pressure_full)
    results.append(
        pressure_core
        - pressure_rate * (spread + (pressure_core - previous[1:-1, 1:-1, :]) / bulk_time)
    )
    return jnp.stack(results)


def dft_table(row_count, col_count, period):
    row_index = jnp.arange(row_count, dtype=jnp.int32)[:, None]
    col_index = jnp.arange(col_count, dtype=jnp.int32)[None, :]
    angles = (row_index * col_index % period).astype(jnp.float32) * (2.0 * math.pi / period)
    return (jnp.cos(angles), jnp.sin(angles))


def combine(plain_part, turned, orientation):
    real_part = plain_part[:, :, 0] - orientation * turned[:, :, 1]
    imag_part = plain_part[:, :, 1] + orientation * turned[:, :, 0]
    return jnp.stack([real_part, imag_part], axis=2)


def transform(columns, orientation):
    length = columns.shape[0]
    width_cols = columns.shape[2]
    inner_size = math.gcd(length, 128)
    outer_size = length // inner_size
    blocks = columns.reshape(inner_size, outer_size, 2, width_cols)
    cosine_table, sine_table = dft_table(inner_size, inner_size, inner_size)
    plain_part = jnp.einsum("bajm,bk->kajm", blocks, cosine_table, precision=highest)
    turned = jnp.einsum("bajm,bk->kajm", blocks, sine_table, precision=highest)
    blocks = combine(plain_part, turned, orientation)
    twist_cos, twist_sin = dft_table(inner_size, outer_size, length)
    twist_cos = twist_cos[:, :, None]
    twist_sin = twist_sin[:, :, None]
    real_part = blocks[:, :, 0]
    imag_part = blocks[:, :, 1]
    blocks = jnp.stack(
        [
            real_part * twist_cos - orientation * imag_part * twist_sin,
            imag_part * twist_cos + orientation * real_part * twist_sin,
        ],
        axis=2,
    )
    cosine_table, sine_table = dft_table(outer_size, outer_size, outer_size)
    plain_part = jnp.einsum("kajm,al->lkjm", blocks, cosine_table, precision=highest)
    turned = jnp.einsum("kajm,al->lkjm", blocks, sine_table, precision=highest)
    return combine(plain_part, turned, orientation).reshape(length, 2, width_cols)


def centered_wave(index_of, length):
    shifted = jnp.where(index_of < length // 2, index_of, index_of - length)
    return shifted.astype(jnp.float32) * (2.0 * math.pi / length)


def forward_rows(loaded, mode_count, groups):
    lateral = loaded.shape[2]
    local_modes = mode_count // groups
    cosine_table, sine_table = dft_table(lateral, mode_count, lateral)
    cos_blocks = cosine_table.reshape(lateral, groups, local_modes)
    sin_blocks = sine_table.reshape(lateral, groups, local_modes)
    real_part = jnp.einsum("zxy,ygk->gxzk", loaded, cos_blocks, precision=highest)
    imag_part = -jnp.einsum("zxy,ygk->gxzk", loaded, sin_blocks, precision=highest)
    return jnp.stack([real_part, imag_part], axis=2).reshape(groups, -1)


def fold_depth(received, mode_count, groups, width_cells, depth_cells):
    local_modes = mode_count // groups
    total_x = groups * width_cells
    columns = received.reshape(total_x, 2, depth_cells * local_modes)
    spectrum = transform(columns, -1.0).reshape(total_x, 2, depth_cells, local_modes)
    index_x = jnp.arange(total_x, dtype=jnp.int32)
    index_y = lax.axis_index("gx") * local_modes + jnp.arange(local_modes, dtype=jnp.int32)
    wave_x = centered_wave(index_x, total_x)
    wave_y = centered_wave(index_y, NY)
    magnitude = jnp.sqrt(wave_x[:, None] ** 2 + wave_y[None, :] ** 2)
    depth_of = (
        lax.axis_index("gz") * depth_cells + jnp.arange(depth_cells, dtype=jnp.int32)
    ).astype(jnp.float32)
    depth_of = (depth_of + 0.5) * layer_depth
    retained = (
        (index_y != NY // 2)[None, :]
        & jnp.logical_not((index_x == 0)[:, None] & (index_y == 0)[None, :])
    ).astype(jnp.float32)
    weights = (
        gravity_scale
        * layer_depth
        * jnp.exp(-magnitude[:, None, :] * depth_of[None, :, None])
        * retained[:, None, :]
    )
    partial_value = jnp.sum(weights[:, None] * spectrum, axis=2)
    summed = lax.psum(partial_value, "gz")
    restored = transform(summed, 1.0)
    return restored.reshape(groups, width_cells * 2 * local_modes)


def finish(returned, mode_count, groups, width_cells):
    local_modes = mode_count // groups
    columns = returned.reshape(groups, width_cells, 2, local_modes)
    mode_index = jnp.arange(mode_count, dtype=jnp.int32)
    factor = jnp.where(mode_index == 0, 1.0, 1.0)
    cosine_table, sine_table = dft_table(mode_count, NY, NY)
    cos_blocks = (factor[:, None] * cosine_table).reshape(groups, local_modes, NY)
    sin_blocks = (factor[:, None] * sine_table).reshape(groups, local_modes, NY)
    real_sum = jnp.einsum("sxk,sky->xy", columns[:, :, 0], cos_blocks, precision=highest)
    imag_sum = jnp.einsum("sxk,sky->xy", columns[:, :, 1], sin_blocks, precision=highest)
    return (real_sum - imag_sum) / (groups * width_cells * NY)


def body(phases, velocity, pressure, density_table, viscosity_table):
    classes = jnp.arange(density_table.shape[0], dtype=jnp.int32)[:, None, None, None]
    chosen = phases[None] == classes
    density = jnp.sum(jnp.where(chosen, density_table[:, None, None, None], 0.0), axis=0)
    viscosity = jnp.sum(jnp.where(chosen, viscosity_table[:, None, None, None], 0.0), axis=0)
    effective = 1.0 / (1.0 / viscosity + 1.0 / shear_time)
    depth_cells, width_cells, lateral = pressure.shape
    groups = lax.axis_size("gx")
    fields = jnp.concatenate([velocity, pressure[None]], axis=0)
    margin = ((1, 1), (1, 1), (0, 0))
    for sweeps in range(ITERS):
        stacked = jnp.concatenate([fields, effective[None]], axis=0)
        widened = with_halo(stacked, (("gx", 2), ("gz", 1)), 1)
        fields = relaxation(
            widened[:4], widened[4], jnp.pad(density, margin), jnp.pad(pressure, margin)
        )
    velocity_out = fields[:3]
    pressure_out = fields[3]
    loaded = density * (1.0 + squeeze * pressure_out)
    packed = forward_rows(loaded, lateral, groups)
    received = lax.all_to_all(packed, "gx", split_axis=0, concat_axis=0, tiled=True)
    folded = fold_depth(received, lateral, groups, width_cells, depth_cells)
    returned = lax.all_to_all(folded, "gx", split_axis=0, concat_axis=0, tiled=True)
    gravity = finish(returned, lateral, groups, width_cells)
    return (velocity_out, pressure_out, gravity)


HALF_MODES = NY // 2
MESH = pl.DeviceIdType.MESH


def split_table(table):
    high = table.astype(jnp.bfloat16)
    low = (table - high.astype(np.float32)).astype(jnp.bfloat16)
    return high, low


def host_tables(groups, width, total_x):
    y = np.arange(NY)[:, None]
    k = np.arange(HALF_MODES)[None, :]
    angle = (y * k % NY) * (2.0 * np.pi / NY)
    along_y = np.concatenate([np.cos(angle), -np.sin(angle)], axis=1).astype(np.float32)
    kx = np.arange(total_x)[:, None]
    local = np.arange(width)[None, :]
    angle = (kx * local % total_x) * (2.0 * np.pi / total_x)
    c, s = np.cos(angle), np.sin(angle)
    along_x = np.block([[c, s], [-s, c]]).astype(np.float32)
    high, low = split_table(along_x)
    along_x = np.concatenate([high, high, low], axis=1)
    angle = (kx * np.arange(groups)[None, :] * width % total_x) * (2.0 * np.pi / total_x)
    phase = np.stack([np.cos(angle).T, np.sin(angle).T]).astype(np.float32)
    x = np.arange(total_x)[None, :]
    angle = (kx * x % total_x) * (2.0 * np.pi / total_x)
    c = np.cos(angle).reshape(total_x, groups, 1, width)
    s = np.sin(angle).reshape(total_x, groups, 1, width)
    back_x = np.concatenate(
        [np.concatenate([c, s], axis=2), np.concatenate([-s, c], axis=2)], axis=0
    ).reshape(2 * total_x, groups * 2 * width).astype(np.float32)
    return split_table(along_y), along_x, phase, split_table(back_x)


def split_value(value):
    high = value.astype(jnp.bfloat16)
    low = (value - high.astype(jnp.float32)).astype(jnp.bfloat16)
    return high, low


def dot(left, right):
    return jnp.dot(left, right, preferred_element_type=jnp.float32)


def dot_turned(left, right):
    return lax.dot_general(
        left, right, (((1,), (1,)), ((), ())), preferred_element_type=jnp.float32
    )


def wave_of(index, length):
    shifted = jnp.where(index < length // 2, index, index - length)
    return shifted.astype(jnp.float32) * (2.0 * math.pi / length)


def new_plane(z, src, eta, low, high, eta_low, eta_high, density, inverse, start):
    width, lateral = density.shape[1:]
    row = lax.broadcasted_iota(jnp.int32, (width, lateral), 0)
    lane = lax.broadcasted_iota(jnp.int32, (width, lateral), 1)
    first_row, last_row = row == 0, row == width - 1
    first_lane, last_lane = lane == 0, lane == lateral - 1

    def around(plane, below, above, row_low, row_high):
        return (
            jnp.where(last_row, row_high, pltpu.roll(plane, width - 1, 0)),
            jnp.where(first_row, row_low, pltpu.roll(plane, 1, 0)),
            jnp.where(last_lane, 0.0, pltpu.roll(plane, lateral - 1, 1)),
            jnp.where(first_lane, 0.0, pltpu.roll(plane, 1, 1)),
            above,
            below,
        )

    eta_c = eta(z + 1)
    faces = [
        eta_c + n
        for n in around(eta_c, eta(z), eta(z + 2), eta_low[pl.ds(z, 1), :], eta_high[pl.ds(z, 1), :])
    ]
    total_face = sum(faces[1:], faces[0])
    values, sides = [], []
    for f in range(4):
        plane = src[f, z + 1]
        values.append(plane)
        sides.append(
            around(plane, src[f, z], src[f, z + 2], low[f, pl.ds(z, 1), :], high[f, pl.ds(z, 1), :])
        )
    pressure_sides = sides[3]
    rate = (0.5 * velocity_rate) * inverse[z]
    results = []
    spread = None
    for f in range(3):
        flux = faces[0] * sides[f][0]
        for n in range(1, 6):
            flux = flux + faces[n] * sides[f][n]
        forcing = flux - total_face * values[f]
        forcing = forcing - (pressure_sides[2 * f] - pressure_sides[2 * f + 1])
        if f == 2:
            forcing = forcing - 2.0 * density[z]
        results.append(values[f] + rate * forcing)
        change = sides[f][2 * f] - sides[f][2 * f + 1]
        spread = change if spread is None else spread + change
    results.append(
        values[3]
        - pressure_rate * (0.5 * spread + (values[3] - start(z)) / bulk_time)
    )
    return results


def kernel(
    groups, layers,
    dens_ref, visc_ref, phases_hbm, velocity_hbm, pressure_hbm,
    ty_high_hbm, ty_low_hbm, along_x, phase, bx_high_hbm, bx_low_hbm,
    velocity_out, pressure_out, gravity,
    ph, fields, middle, result, density, inverse,
    send_low, send_high, get_low, get_high, send_low2, send_high2, get_low2, get_high2,
    ty_high, ty_low, bx_high, bx_low,
    loaded, partial, got_z, mine, got_x, back, got_back,
    load_sem, z_sem, x_sem, pair_sem, out_sem, send_sem, recv_sem, send_sem2, recv_sem2,
):
    model, gx, gz = lax.axis_index("models"), lax.axis_index("gx"), lax.axis_index("gz")
    depth, width, lateral = density.shape
    total_x = groups * width
    ranks = groups * layers
    rank = gx * layers + gz

    loads = [
        pltpu.make_async_copy(src, dst, load_sem.at[i])
        for i, (src, dst) in enumerate(
            [
                (phases_hbm, ph),
                (velocity_hbm, fields.at[pl.ds(0, 3), pl.ds(1, depth)]),
                (pressure_hbm, fields.at[3, pl.ds(1, depth)]),
                (ty_high_hbm, ty_high),
                (ty_low_hbm, ty_low),
                (bx_high_hbm, bx_high),
                (bx_low_hbm, bx_low),
            ]
        )
    ]
    for copy in loads:
        copy.start()

    barrier = pltpu.get_barrier_semaphore()
    for j in range(1, ranks):
        other = lax.rem(rank + j, ranks)
        pl.semaphore_signal(
            barrier, inc=1, device_id=(model, other // layers, lax.rem(other, layers)),
            device_id_type=MESH,
        )

    edge = (depth + 1) * gz
    for f in range(5):
        fields[f, edge] = jnp.zeros((width, lateral), jnp.float32)
    for f in range(4):
        middle[f, edge] = jnp.zeros((width, lateral), jnp.float32)

    @pl.when(gx == 0)
    def _():
        get_low[...] = jnp.zeros_like(get_low)
        get_low2[...] = jnp.zeros_like(get_low2)

    @pl.when(gx == groups - 1)
    def _():
        get_high[...] = jnp.zeros_like(get_high)
        get_high2[...] = jnp.zeros_like(get_high2)

    loads[0].wait()

    def look_up(z, carry):
        kind = ph[z]
        dens = jnp.full(kind.shape, dens_ref[0], jnp.float32)
        visc = jnp.full(kind.shape, visc_ref[0], jnp.float32)
        for c in range(1, dens_ref.shape[0]):
            here = kind == c
            dens = jnp.where(here, dens_ref[c], dens)
            visc = jnp.where(here, visc_ref[c], visc)
        inv = 1.0 / visc + 1.0 / shear_time
        density[z] = dens
        inverse[z] = inv
        fields[4, z + 1] = 1.0 / inv
        return carry

    lax.fori_loop(0, depth, look_up, 0)
    loads[1].wait()
    loads[2].wait()

    def exchange(stage, block, count, out_low, out_high, in_low, in_high):
        for f in range(count):
            out_low[f] = block[f, 1 : depth + 1, 0, :]
            out_high[f] = block[f, 1 : depth + 1, width - 1, :]
        across = pltpu.make_async_remote_copy(
            src_ref=block.at[:, depth - (depth - 1) * gz],
            dst_ref=block.at[:, edge],
            send_sem=z_sem.at[2 * stage],
            recv_sem=z_sem.at[2 * stage + 1],
            device_id=(model, gx, 1 - gz),
            device_id_type=MESH,
        )
        downward = pltpu.make_async_remote_copy(
            src_ref=out_low, dst_ref=in_high,
            send_sem=x_sem.at[4 * stage], recv_sem=x_sem.at[4 * stage + 1],
            device_id=(model, lax.rem(gx + groups - 1, groups), gz), device_id_type=MESH,
        )
        upward = pltpu.make_async_remote_copy(
            src_ref=out_high, dst_ref=in_low,
            send_sem=x_sem.at[4 * stage + 2], recv_sem=x_sem.at[4 * stage + 3],
            device_id=(model, lax.rem(gx + 1, groups), gz), device_id_type=MESH,
        )
        if stage == 0:
            pl.semaphore_wait(barrier, ranks - 1)

        @pl.when(gx > 0)
        def _():
            downward.start()

        @pl.when(gx < groups - 1)
        def _():
            upward.start()

        across.start()

        across.wait()

        @pl.when(gx > 0)
        def _():
            downward.wait_send()
            upward.wait_recv()

        @pl.when(gx < groups - 1)
        def _():
            upward.wait_send()
            downward.wait_recv()

    def eta(index):
        return fields[4, index]

    def start(z):
        return fields[3, z + 1]

    eta_low, eta_high = get_low.at[4], get_high.at[4]
    exchange(0, fields, 5, send_low, send_high, get_low, get_high)

    def first(z, carry):
        values = new_plane(
            z, fields, eta, get_low, get_high, eta_low, eta_high, density, inverse, start
        )
        for f in range(4):
            middle[f, z + 1] = values[f]
        return carry

    lax.fori_loop(0, depth, first, 0)
    exchange(1, middle, 4, send_low2, send_high2, get_low2, get_high2)

    def second(z, carry):
        values = new_plane(
            z, middle, eta, get_low2, get_high2, eta_low, eta_high, density, inverse, start
        )
        for f in range(4):
            result[f, z] = values[f]
        loaded[z] = density[z] * (1.0 + squeeze * values[3])
        return carry

    lax.fori_loop(0, depth, second, 0)
    outs = [
        pltpu.make_async_copy(result.at[pl.ds(0, 3)], velocity_out, out_sem.at[0]),
        pltpu.make_async_copy(result.at[3], pressure_out, out_sem.at[1]),
    ]
    for copy in outs:
        copy.start()

    loads[3].wait()
    loads[4].wait()
    high, low = split_value(loaded[...].reshape(depth * width, lateral))
    both = dot(jnp.concatenate([high, low], axis=0), ty_high[...])
    rows = both[: depth * width] + both[depth * width :] + dot(high, ty_low[...])

    index_x = lax.broadcasted_iota(jnp.int32, (total_x, HALF_MODES), 0)
    index_y = lax.broadcasted_iota(jnp.int32, (total_x, HALF_MODES), 1)
    wx, wy = wave_of(index_x, total_x), wave_of(index_y, NY)
    magnitude = jnp.sqrt(wx * wx + wy * wy)
    decay = jnp.exp(-layer_depth * magnitude)
    decay = jnp.concatenate([decay, decay], axis=0)
    weights = along_x[...]
    total = None
    for z in range(depth - 1, -1, -1):
        layer = rows[z * width : (z + 1) * width]
        layer = jnp.concatenate([layer[:, :HALF_MODES], layer[:, HALF_MODES:]], axis=0)
        high, low = split_value(layer)
        spectrum = dot(weights, jnp.concatenate([high, low, high], axis=0))
        total = spectrum if total is None else total * decay + spectrum
    above = jnp.exp(-(layer_depth * depth) * magnitude * gz.astype(jnp.float32))
    real = jnp.transpose(total[:total_x] * above)
    imag = jnp.transpose(total[total_x:] * above)
    cos_row, sin_row = phase[0, pl.ds(gx, 1), :], phase[1, pl.ds(gx, 1), :]
    partial[:, :total_x] = real * cos_row + imag * sin_row
    partial[:, total_x:] = imag * cos_row - real * sin_row

    held = HALF_MODES // layers
    across = pltpu.make_async_remote_copy(
        src_ref=partial.at[pl.ds(pl.multiple_of(held * (1 - gz), held), held)],
        dst_ref=got_z,
        send_sem=pair_sem.at[0], recv_sem=pair_sem.at[1],
        device_id=(model, gx, 1 - gz), device_id_type=MESH,
    )
    across.start()
    across.wait()
    own = held // groups
    mine[...] = partial[pl.ds(pl.multiple_of(held * gz, held), held)] + got_z[...]

    copies = []
    for j in range(1, groups):
        target = lax.rem(gx + j, groups)
        copy = pltpu.make_async_remote_copy(
            src_ref=mine.at[pl.ds(pl.multiple_of(target * own, own), own)],
            dst_ref=got_x.at[gx],
            send_sem=send_sem.at[j], recv_sem=recv_sem.at[j],
            device_id=(model, target, gz), device_id_type=MESH,
        )
        copy.start()
        copies.append(copy)
    index_x = lax.broadcasted_iota(jnp.int32, (own, total_x), 1)
    index_y = lax.broadcasted_iota(jnp.int32, (own, total_x), 0) + (held * gz + own * gx)
    wx, wy = wave_of(index_x, total_x), wave_of(index_y, NY)
    scale = gravity_scale * layer_depth / (total_x * NY)
    weight = scale * jnp.exp((-0.5 * layer_depth) * jnp.sqrt(wx * wx + wy * wy))
    weight = weight * jnp.where(index_y == 0, jnp.where(index_x == 0, 0.0, 1.0), 2.0)
    weight = jnp.concatenate([weight, weight], axis=1)
    summed = mine[pl.ds(pl.multiple_of(gx * own, own), own)]
    for j in range(1, groups):
        copies[j - 1].wait_recv()
        summed = summed + got_x[lax.rem(gx + groups - j, groups)]
    loads[5].wait()
    loads[6].wait()
    high, low = split_value(summed * weight)
    both = dot(jnp.concatenate([high, low], axis=0), bx_high[...])
    columns = both[:own] + both[own:] + dot(high, bx_low[...])
    for part in range(2 * total_x // 128):
        back[part] = columns[:, 128 * part : 128 * (part + 1)]

    per_part = 128 // (2 * width)
    slot = gz * groups + gx
    returns = []
    for j in range(1, ranks):
        other = lax.rem(rank + j, ranks)
        copy = pltpu.make_async_remote_copy(
            src_ref=back.at[(other // layers) // per_part],
            dst_ref=got_back.at[slot],
            send_sem=send_sem2.at[j], recv_sem=recv_sem2.at[j],
            device_id=(model, other // layers, lax.rem(other, layers)), device_id_type=MESH,
        )
        copy.start()
        returns.append(copy)
    got_back[slot] = back[gx // per_part]
    for copy in returns:
        copy.wait_recv()
    waves = got_back[...].reshape(HALF_MODES, 128)
    waves = pltpu.roll(waves, lax.rem(128 - 2 * width * lax.rem(gx, per_part), 128), 1)
    waves = jnp.transpose(waves)
    waves = jnp.concatenate([waves[:width], waves[width : 2 * width]], axis=1)
    high, low = split_value(waves)
    both = dot_turned(jnp.concatenate([high, low], axis=0), ty_high[...])
    gravity[...] = both[:width] + both[width:] + dot_turned(high, ty_low[...])

    for copy in copies + returns:
        copy.wait_send()
    for copy in outs:
        copy.wait()


def fused_body(phases, velocity, pressure, density_table, viscosity_table):
    depth, width, lateral = pressure.shape
    groups, layers = lax.axis_size("gx"), lax.axis_size("gz")
    total_x = groups * width
    ty, along_x, phase, bx = host_tables(groups, width, total_x)
    held = HALF_MODES // layers
    own = held // groups
    ranks = groups * layers
    f32, b16 = jnp.float32, jnp.bfloat16
    vmem = pl.BlockSpec(memory_space=pltpu.VMEM)
    smem = pl.BlockSpec(memory_space=pltpu.SMEM)
    anywhere = pl.BlockSpec(memory_space=pl.ANY)
    rows5, rows4 = pltpu.VMEM((5, depth, lateral), f32), pltpu.VMEM((4, depth, lateral), f32)
    cells = (depth, width, lateral)
    sems = pltpu.SemaphoreType.DMA
    return pl.pallas_call(
        functools.partial(kernel, groups, layers),
        out_shape=(
            jax.ShapeDtypeStruct(velocity.shape, f32),
            jax.ShapeDtypeStruct(pressure.shape, f32),
            jax.ShapeDtypeStruct((width, lateral), f32),
        ),
        in_specs=[smem, smem] + [anywhere] * 5 + [vmem] * 2 + [anywhere] * 2,
        out_specs=(anywhere, anywhere, vmem),
        scratch_shapes=[
            pltpu.VMEM(cells, jnp.int32),
            pltpu.VMEM((5, depth + 2, width, lateral), f32),
            pltpu.VMEM((4, depth + 2, width, lateral), f32),
            pltpu.VMEM((4,) + cells, f32),
            pltpu.VMEM(cells, f32),
            pltpu.VMEM(cells, f32),
            rows5, rows5, rows5, rows5, rows4, rows4, rows4, rows4,
            pltpu.VMEM(ty[0].shape, b16),
            pltpu.VMEM(ty[0].shape, b16),
            pltpu.VMEM(bx[0].shape, b16),
            pltpu.VMEM(bx[0].shape, b16),
            pltpu.VMEM(cells, f32),
            pltpu.VMEM((HALF_MODES, 2 * total_x), f32),
            pltpu.VMEM((held, 2 * total_x), f32),
            pltpu.VMEM((held, 2 * total_x), f32),
            pltpu.VMEM((groups, own, 2 * total_x), f32),
            pltpu.VMEM((2 * total_x // 128, own, 128), f32),
            pltpu.VMEM((ranks, own, 128), f32),
            sems((7,)), sems((4,)), sems((8,)), sems((2,)), sems((2,)),
            sems((groups,)), sems((groups,)), sems((ranks,)), sems((ranks,)),
        ],
        compiler_params=pltpu.CompilerParams(
            collective_id=0, has_side_effects=True, vmem_limit_bytes=40 * 1024 * 1024
        ),
    )(
        density_table, viscosity_table, phases, velocity, pressure,
        jnp.asarray(ty[0]), jnp.asarray(ty[1]), jnp.asarray(along_x), jnp.asarray(phase),
        jnp.asarray(bx[0]), jnp.asarray(bx[1]),
    )


def local_program(phases, velocity, pressure, density_table, viscosity_table):
    depth, width, lateral = pressure.shape
    groups, layers = lax.axis_size("gx"), lax.axis_size("gz")
    fits = layers == 2 and groups * width == 128 and width == 16 and depth % 8 == 0
    chosen = fused_body if fits else body
    return chosen(phases, velocity, pressure, density_table, viscosity_table)


def solution(mesh):
    in_specs = (
        P(("models", "gz"), "gx", None),
        P(None, ("models", "gz"), "gx", None),
        P(("models", "gz"), "gx", None),
        P(),
        P(),
    )
    out_specs = (
        P(None, ("models", "gz"), "gx", None),
        P(("models", "gz"), "gx", None),
        P(("models", "gx"), None),
    )
    return jax.shard_map(local_program, mesh=mesh, in_specs=in_specs, out_specs=out_specs, check_vma=False)
```

profile of v0, /device:TPU:0, one launch (start us, length us, event | category | flops | bytes accessed | tf_op | source)
XLA Modules:
  0.0 45.7 jit_solution(18365131405360053529)
XLA Ops:
  0.6 0.0 copy-start
  0.6 1.1 %copy-done = f32[3,8,16,512]{3,2,1,0:T(8,128)S(1)} copy-done((f32[3,8,16,512]{3,2,1,0:T(8,128)S(1)}, f32[3,8,16,512]{3,2,1,0:T(8,128)}, u32[]{:S(2)}) %copy-start) | copy-done | bytes 786456
  1.8 0.0 copy-start.1
  1.8 1.0 %copy-done.1 = bf16[512,512]{1,0:T(8,128)(2,1)S(1)} copy-done((bf16[512,512]{1,0:T(8,128)(2,1)S(1)}, bf16[512,512]{1,0:T(8,128)(2,1)}, u32[]{:S(2)}) %copy-start.1) | copy-done | bytes 524312
  2.8 0.0 copy-start.2
  2.8 1.0 %copy-done.2 = bf16[512,512]{1,0:T(8,128)(2,1)S(1)} copy-done((bf16[512,512]{1,0:T(8,128)(2,1)S(1)}, bf16[512,512]{1,0:T(8,128)(2,1)}, u32[]{:S(2)}) %copy-start.2) | copy-done | bytes 524312
  3.9 0.0 copy-start.3
  3.9 0.9 %copy-done.3 = s32[8,16,512]{2,1,0:T(8,128)S(1)} copy-done((s32[8,16,512]{2,1,0:T(8,128)S(1)}, s32[8,16,512]{2,1,0:T(8,128)}, u32[]{:S(2)}) %copy-start.3) | copy-done | bytes 262168
  4.8 0.0 copy-start.4
  4.8 0.9 %copy-done.4 = f32[8,16,512]{2,1,0:T(8,128)S(1)} copy-done((f32[8,16,512]{2,1,0:T(8,128)S(1)}, f32[8,16,512]{2,1,0:T(8,128)}, u32[]{:S(2)}) %copy-start.4) | copy-done | bytes 262168
  5.8 0.0 copy-start.5
  5.8 0.9 %copy-done.5 = bf16[256,256]{1,0:T(8,128)(2,1)S(1)} copy-done((bf16[256,256]{1,0:T(8,128)(2,1)S(1)}, bf16[256,256]{1,0:T(8,128)(2,1)}, u32[]{:S(2)}) %copy-start.5) | copy-done | bytes 131096
  6.7 0.0 copy-start.6
  6.7 0.9 %copy-done.6 = bf16[256,256]{1,0:T(8,128)(2,1)S(1)} copy-done((bf16[256,256]{1,0:T(8,128)(2,1)S(1)}, bf16[256,256]{1,0:T(8,128)(2,1)}, u32[]{:S(2)}) %copy-start.6) | copy-done | bytes 131096
  7.6 0.0 copy-start.7
  7.6 0.8 %copy-done.7 = bf16[256,96]{1,0:T(8,128)(2,1)S(1)} copy-done((bf16[256,96]{1,0:T(8,128)(2,1)S(1)}, bf16[256,96]{1,0:T(8,128)(2,1)}, u32[]{:S(2)}) %copy-start.7) | copy-done | bytes 49176
  8.4 0.0 copy-start.8
  8.4 0.7 %copy-done.8 = f32[2,8,128]{2,1,0:T(8,128)S(1)} copy-done((f32[2,8,128]{2,1,0:T(8,128)S(1)}, f32[2,8,128]{2,1,0:T(8,128)}, u32[]{:S(2)}) %copy-start.8) | copy-done | bytes 8216
  9.1 0.0 copy-start.9
  9.1 0.7 %copy-done.9 = f32[8]{0:T(128)S(1)} copy-done((f32[8]{0:T(128)S(1)}, f32[8]{0:T(128)}, u32[]{:S(2)}) %copy-start.9) | copy-done | bytes 56
  9.8 0.0 copy-start.10
  9.8 0.7 %copy-done.10 = f32[8]{0:T(128)S(1)} copy-done((f32[8]{0:T(128)S(1)}, f32[8]{0:T(128)}, u32[]{:S(2)}) %copy-start.10) | copy-done | bytes 56
  10.4 33.0 %shard_map.130 = (f32[3,8,16,512]{3,2,1,0:T(8,128)S(1)}, f32[8,16,512]{2,1,0:T(8,128)S(1)}, f32[16,512]{1,0:T(8,128)S(1)}) custom-call(f32[8]{0:T(128)S(1)} %copy-done.9, f32[8]{0:T(128)S(1)} %copy-done.10, s32[8,16,512]{2,1,0:T(8,128)S(1)} %copy-done.3, f32[3,8,16,512]{3,2,1,0:T(8,128)S(1)} %copy-done, f32[8,16,512]{2,1,0:T(8,128)S(1)} %copy-done.4, ...), custom_call_target="tpu_custom_call" | custom-call | tf_op jit(solution)/shard_map/pallas_call | solution.py:595
  43.5 0.9 %copy.17 = f32[3,8,16,512]{3,2,1,0:T(8,128)} copy(f32[3,8,16,512]{3,2,1,0:T(8,128)S(1)} %get-tuple-element.6) | data formatting | bytes 1572864
  44.3 0.7 %copy.18 = f32[8,16,512]{2,1,0:T(8,128)} copy(f32[8,16,512]{2,1,0:T(8,128)S(1)} %get-tuple-element.7) | data formatting | bytes 524288
  45.0 0.6 %copy.19 = f32[16,512]{1,0:T(8,128)} copy(f32[16,512]{1,0:T(8,128)S(1)} %get-tuple-element.8) | data formatting | bytes 65536
Async XLA Ops:
  0.6 1.1 %copy-start = (f32[3,8,16,512]{3,2,1,0:T(8,128)S(1)}, f32[3,8,16,512]{3,2,1,0:T(8,128)}, u32[]{:S(2)}) copy-start(f32[3,8,16,512]{3,2,1,0:T(8,128)} %velocity_hbm.1) | copy-start | bytes 2359300
  1.8 1.0 %copy-start.1 = (bf16[512,512]{1,0:T(8,128)(2,1)S(1)}, bf16[512,512]{1,0:T(8,128)(2,1)}, u32[]{:S(2)}) copy-start(bf16[512,512]{1,0:T(8,128)(2,1)} %constant.13.clone.ty_low_hbm) | copy-start | bytes 1572868
  2.8 1.0 %copy-start.2 = (bf16[512,512]{1,0:T(8,128)(2,1)S(1)}, bf16[512,512]{1,0:T(8,128)(2,1)}, u32[]{:S(2)}) copy-start(bf16[512,512]{1,0:T(8,128)(2,1)} %constant.12.clone.ty_high_hbm) | copy-start | bytes 1572868
  3.9 0.9 %copy-start.3 = (s32[8,16,512]{2,1,0:T(8,128)S(1)}, s32[8,16,512]{2,1,0:T(8,128)}, u32[]{:S(2)}) copy-start(s32[8,16,512]{2,1,0:T(8,128)} %phases_hbm.1) | copy-start | bytes 786436
  4.8 0.9 %copy-start.4 = (f32[8,16,512]{2,1,0:T(8,128)S(1)}, f32[8,16,512]{2,1,0:T(8,128)}, u32[]{:S(2)}) copy-start(f32[8,16,512]{2,1,0:T(8,128)} %pressure_hbm.1) | copy-start | bytes 786436
  5.8 0.9 %copy-start.5 = (bf16[256,256]{1,0:T(8,128)(2,1)S(1)}, bf16[256,256]{1,0:T(8,128)(2,1)}, u32[]{:S(2)}) copy-start(bf16[256,256]{1,0:T(8,128)(2,1)} %constant.17.clone.bx_low_hbm) | copy-start | bytes 393220
  6.7 0.9 %copy-start.6 = (bf16[256,256]{1,0:T(8,128)(2,1)S(1)}, bf16[256,256]{1,0:T(8,128)(2,1)}, u32[]{:S(2)}) copy-start(bf16[256,256]{1,0:T(8,128)(2,1)} %constant.16.clone.bx_high_hbm) | copy-start | bytes 393220
  7.6 0.8 %copy-start.7 = (bf16[256,96]{1,0:T(8,128)(2,1)S(1)}, bf16[256,96]{1,0:T(8,128)(2,1)}, u32[]{:S(2)}) copy-start(bf16[256,96]{1,0:T(8,128)(2,1)} %constant.14.clone.along_x) | copy-start | bytes 147460
  8.4 0.7 %copy-start.8 = (f32[2,8,128]{2,1,0:T(8,128)S(1)}, f32[2,8,128]{2,1,0:T(8,128)}, u32[]{:S(2)}) copy-start(f32[2,8,128]{2,1,0:T(8,128)} %constant.15.clone.phase) | copy-start | bytes 24580
  9.1 0.7 %copy-start.9 = (f32[8]{0:T(128)S(1)}, f32[8]{0:T(128)}, u32[]{:S(2)}) copy-start(f32[8]{0:T(128)} %dens_ref.1) | copy-start | bytes 100
  9.8 0.7 %copy-start.10 = (f32[8]{0:T(128)S(1)}, f32[8]{0:T(128)}, u32[]{:S(2)}) copy-start(f32[8]{0:T(128)} %visc_ref.1) | copy-start | bytes 100
where the time goes:
time: 46.1 us; the launch traced here: 45.7 us
  Pallas kernels  33 us (72%)
  local copies, waits for them, and re-layouts  12 us (26%)
  between operations  0.66 us (1%)
    pallas_call x1, Pallas kernels, fused_body(): pl.pallas_call(functools.partial(kernel, groups, layers), out_shape=(jax....  33 us
    unnamed x25, local copies, waits for them, and re-layouts  12 us

commit v1 on v0

--- a/solution.py
+++ b/solution.py
@@ -219,9 +219,9 @@
     return high, low
 
 
-def host_tables(groups, width, total_x):
+def host_tables(groups, layers, width, total_x):
     y = np.arange(NY)[:, None]
-    k = np.arange(HALF_MODES)[None, :]
+    k = mode_at(np.arange(HALF_MODES), groups * layers)[None, :]
     angle = (y * k % NY) * (2.0 * np.pi / NY)
     along_y = np.concatenate([np.cos(angle), -np.sin(angle)], axis=1).astype(np.float32)
     kx = np.arange(total_x)[:, None]
@@ -240,7 +240,11 @@
     back_x = np.concatenate(
         [np.concatenate([c, s], axis=2), np.concatenate([-s, c], axis=2)], axis=0
     ).reshape(2 * total_x, groups * 2 * width).astype(np.float32)
-    return split_table(along_y), along_x, phase, split_table(back_x)
+    return np.stack(split_table(along_y)), along_x, phase, np.stack(split_table(back_x))
+
+
+def mode_at(place, owners):
+    return place % (8 * owners) // 8 * 16 + place // (8 * owners) * 8 + place % 8
 
 
 def split_value(value):
@@ -264,38 +268,9 @@
     return shifted.astype(jnp.float32) * (2.0 * math.pi / length)
 
 
-def new_plane(z, src, eta, low, high, eta_low, eta_high, density, inverse, start):
-    width, lateral = density.shape[1:]
-    row = lax.broadcasted_iota(jnp.int32, (width, lateral), 0)
-    lane = lax.broadcasted_iota(jnp.int32, (width, lateral), 1)
-    first_row, last_row = row == 0, row == width - 1
-    first_lane, last_lane = lane == 0, lane == lateral - 1
-
-    def around(plane, below, above, row_low, row_high):
-        return (
-            jnp.where(last_row, row_high, pltpu.roll(plane, width - 1, 0)),
-            jnp.where(first_row, row_low, pltpu.roll(plane, 1, 0)),
-            jnp.where(last_lane, 0.0, pltpu.roll(plane, lateral - 1, 1)),
-            jnp.where(first_lane, 0.0, pltpu.roll(plane, 1, 1)),
-            above,
-            below,
-        )
-
-    eta_c = eta(z + 1)
-    faces = [
-        eta_c + n
-        for n in around(eta_c, eta(z), eta(z + 2), eta_low[pl.ds(z, 1), :], eta_high[pl.ds(z, 1), :])
-    ]
+def advance(values, sides, faces, density, inverse, start):
     total_face = sum(faces[1:], faces[0])
-    values, sides = [], []
-    for f in range(4):
-        plane = src[f, z + 1]
-        values.append(plane)
-        sides.append(
-            around(plane, src[f, z], src[f, z + 2], low[f, pl.ds(z, 1), :], high[f, pl.ds(z, 1), :])
-        )
-    pressure_sides = sides[3]
-    rate = (0.5 * velocity_rate) * inverse[z]
+    rate = (0.5 * velocity_rate) * inverse
     results = []
     spread = None
     for f in range(3):
@@ -303,47 +278,102 @@
         for n in range(1, 6):
             flux = flux + faces[n] * sides[f][n]
         forcing = flux - total_face * values[f]
-        forcing = forcing - (pressure_sides[2 * f] - pressure_sides[2 * f + 1])
+        forcing = forcing - (sides[3][2 * f] - sides[3][2 * f + 1])
         if f == 2:
-            forcing = forcing - 2.0 * density[z]
+            forcing = forcing - 2.0 * density
         results.append(values[f] + rate * forcing)
         change = sides[f][2 * f] - sides[f][2 * f + 1]
         spread = change if spread is None else spread + change
     results.append(
-        values[3]
-        - pressure_rate * (0.5 * spread + (values[3] - start(z)) / bulk_time)
+        values[3] - pressure_rate * (0.5 * spread + (values[3] - start) / bulk_time)
     )
     return results
+
+
+def beside_y(tile):
+    lateral = tile.shape[1]
+    lane = lax.broadcasted_iota(jnp.int32, tile.shape, 1)
+    return (
+        jnp.where(lane == lateral - 1, 0.0, pltpu.roll(tile, lateral - 1, 1)),
+        jnp.where(lane == 0, 0.0, pltpu.roll(tile, 1, 1)),
+    )
+
+
+def inner_planes(z, block, eta, density, inverse, start):
+    def around(ref, lead):
+        plane = ref[lead + (z + 1,)]
+        width = plane.shape[0]
+        ahead, behind = beside_y(plane)
+        return plane, (
+            pltpu.roll(plane, width - 1, 0), pltpu.roll(plane, 1, 0), ahead, behind,
+            ref[lead + (z + 2,)], ref[lead + (z,)],
+        )
+
+    center, others = around(eta, ())
+    faces = [center + other for other in others]
+    pairs = [around(block, (f,)) for f in range(4)]
+    return advance(
+        [p[0] for p in pairs], [p[1] for p in pairs], faces, density[z], inverse[z], start(z)
+    )
+
+
+def edge_rows(row, block, eta, halo, eta_halo, density, inverse, first):
+    depth = density.shape[0]
+    inward = 1 if row == 0 else -1
+
+    def around(ref, lead, outer):
+        tile = ref[lead + (slice(1, depth + 1), row)]
+        layer = lax.broadcasted_iota(jnp.int32, tile.shape, 0)
+        below = jnp.where(layer == 0, ref[lead + (slice(0, 1), row)], pltpu.roll(tile, 1, 0))
+        above = jnp.where(
+            layer == depth - 1,
+            ref[lead + (slice(depth + 1, depth + 2), row)],
+            pltpu.roll(tile, depth - 1, 0),
+        )
+        ahead, behind = beside_y(tile)
+        inner = ref[lead + (slice(1, depth + 1), row + inward)]
+        along = (inner, outer) if row == 0 else (outer, inner)
+        return tile, along + (ahead, behind, above, below)
+
+    center, others = around(eta, (), eta_halo[...])
+    faces = [center + other for other in others]
+    pairs = [around(block, (f,), halo[f]) for f in range(4)]
+    return advance(
+        [p[0] for p in pairs], [p[1] for p in pairs], faces,
+        density[:, row], inverse[:, row], first[3, 1 : depth + 1, row],
+    )
 
 
 def kernel(
     groups, layers,
     dens_ref, visc_ref, phases_hbm, velocity_hbm, pressure_hbm,
-    ty_high_hbm, ty_low_hbm, along_x, phase, bx_high_hbm, bx_low_hbm,
-    velocity_out, pressure_out, gravity,
-    ph, fields, middle, result, density, inverse,
+    ty_hbm, along_x_hbm, phase_hbm, bx_hbm,
+    result, waves_out,
+    ph, fields, eta, middle, density, inverse,
     send_low, send_high, get_low, get_high, send_low2, send_high2, get_low2, get_high2,
-    ty_high, ty_low, bx_high, bx_low,
+    eta_send_low, eta_send_high, eta_low, eta_high,
+    ty, along_x, phase, bx,
     loaded, partial, got_z, mine, got_x, back, got_back,
-    load_sem, z_sem, x_sem, pair_sem, out_sem, send_sem, recv_sem, send_sem2, recv_sem2,
+    load_sem, z_sem, x_sem, pair_sem, send_sem, recv_sem, send_sem2, recv_sem2,
 ):
     model, gx, gz = lax.axis_index("models"), lax.axis_index("gx"), lax.axis_index("gz")
     depth, width, lateral = density.shape
     total_x = groups * width
     ranks = groups * layers
     rank = gx * layers + gz
+    last = width - 1
 
     loads = [
         pltpu.make_async_copy(src, dst, load_sem.at[i])
         for i, (src, dst) in enumerate(
             [
-                (phases_hbm, ph),
                 (velocity_hbm, fields.at[pl.ds(0, 3), pl.ds(1, depth)]),
                 (pressure_hbm, fields.at[3, pl.ds(1, depth)]),
-                (ty_high_hbm, ty_high),
-                (ty_low_hbm, ty_low),
-                (bx_high_hbm, bx_high),
-                (bx_low_hbm, bx_low),
+                (phases_hbm, ph),
+                (ty_hbm, ty),
+                (along_x_hbm, along_x),
+                (phase_hbm, phase),
+                (bx_hbm, bx),
             ]
         )
     ]
@@ -359,22 +389,77 @@
         )
 
     edge = (depth + 1) * gz
-    for f in range(5):
-        fields[f, edge] = jnp.zeros((width, lateral), jnp.float32)
+    empty = jnp.zeros((width, lateral), jnp.float32)
+    eta[edge] = empty
     for f in range(4):
-        middle[f, edge] = jnp.zeros((width, lateral), jnp.float32)
+        fields[f, edge] = empty
+        middle[f, edge] = empty
 
     @pl.when(gx == 0)
     def _():
-        get_low[...] = jnp.zeros_like(get_low)
-        get_low2[...] = jnp.zeros_like(get_low2)
+        for ref in (get_low, get_low2, eta_low):
+            ref[...] = jnp.zeros_like(ref)
 
     @pl.when(gx == groups - 1)
     def _():
-        get_high[...] = jnp.zeros_like(get_high)
-        get_high2[...] = jnp.zeros_like(get_high2)
-
+        for ref in (get_high, get_high2, eta_high):
+            ref[...] = jnp.zeros_like(ref)
+
+    def beside_x(stage, out_low, out_high, in_low, in_high):
+        down = pltpu.make_async_remote_copy(
+            src_ref=out_low, dst_ref=in_high,
+            send_sem=x_sem.at[4 * stage], recv_sem=x_sem.at[4 * stage + 1],
+            device_id=(model, lax.rem(gx + groups - 1, groups), gz), device_id_type=MESH,
+        )
+        up = pltpu.make_async_remote_copy(
+            src_ref=out_high, dst_ref=in_low,
+            send_sem=x_sem.at[4 * stage + 2], recv_sem=x_sem.at[4 * stage + 3],
+            device_id=(model, lax.rem(gx + 1, groups), gz), device_id_type=MESH,
+        )
+
+        @pl.when(gx > 0)
+        def _():
+            down.start()
+
+        @pl.when(gx < groups - 1)
+        def _():
+            up.start()
+
+        return down, up
+
+    def wait_x(pair):
+        down, up = pair
+
+        @pl.when(gx > 0)
+        def _():
+            down.wait_send()
+            up.wait_recv()
+
+        @pl.when(gx < groups - 1)
+        def _():
+            up.wait_send()
+            down.wait_recv()
+
+    def beside_z(stage, source, target):
+        copy = pltpu.make_async_remote_copy(
+            src_ref=source, dst_ref=target,
+            send_sem=z_sem.at[2 * stage], recv_sem=z_sem.at[2 * stage + 1],
+            device_id=(model, gx, 1 - gz), device_id_type=MESH,
+        )
+        copy.start()
+        return copy
+
+    facing = depth - (depth - 1) * gz
     loads[0].wait()
+    loads[1].wait()
+    for f in range(4):
+        send_low[f] = fields[f, 1 : depth + 1, 0]
+        send_high[f] = fields[f, 1 : depth + 1, last]
+    pl.semaphore_wait(barrier, ranks - 1)
+    x_first = beside_x(0, send_low, send_high, get_low, get_high)
+    z_first = beside_z(0, fields.at[:, facing], fields.at[:, edge])
+
+    loads[2].wait()
 
     def look_up(z, carry):
         kind = ph[z]
@@ -387,108 +472,69 @@
         inv = 1.0 / visc + 1.0 / shear_time
         density[z] = dens
         inverse[z] = inv
-        fields[4, z + 1] = 1.0 / inv
+        eta[z + 1] = 1.0 / inv
         return carry
 
     lax.fori_loop(0, depth, look_up, 0)
-    loads[1].wait()
-    loads[2].wait()
-
-    def exchange(stage, block, count, out_low, out_high, in_low, in_high):
-        for f in range(count):
-            out_low[f] = block[f, 1 : depth + 1, 0, :]
-            out_high[f] = block[f, 1 : depth + 1, width - 1, :]
-        across = pltpu.make_async_remote_copy(
-            src_ref=block.at[:, depth - (depth - 1) * gz],
-            dst_ref=block.at[:, edge],
-            send_sem=z_sem.at[2 * stage],
-            recv_sem=z_sem.at[2 * stage + 1],
-            device_id=(model, gx, 1 - gz),
-            device_id_type=MESH,
-        )
-        downward = pltpu.make_async_remote_copy(
-            src_ref=out_low, dst_ref=in_high,
-            send_sem=x_sem.at[4 * stage], recv_sem=x_sem.at[4 * stage + 1],
-            device_id=(model, lax.rem(gx + groups - 1, groups), gz), device_id_type=MESH,
-        )
-        upward = pltpu.make_async_remote_copy(
-            src_ref=out_high, dst_ref=in_low,
-            send_sem=x_sem.at[4 * stage + 2], recv_sem=x_sem.at[4 * stage + 3],
-            device_id=(model, lax.rem(gx + 1, groups), gz), device_id_type=MESH,
-        )
-        if stage == 0:
-            pl.semaphore_wait(barrier, ranks - 1)
-
-        @pl.when(gx > 0)
-        def _():
-            downward.start()
-
-        @pl.when(gx < groups - 1)
-        def _():
-            upward.start()
-
-        across.start()
-
-        across.wait()
-
-        @pl.when(gx > 0)
-        def _():
-            downward.wait_send()
-            upward.wait_recv()
-
-        @pl.when(gx < groups - 1)
-        def _():
-            upward.wait_send()
-            downward.wait_recv()
-
-    def eta(index):
-        return fields[4, index]
+    eta_send_low[...] = eta[1 : depth + 1, 0]
+    eta_send_high[...] = eta[1 : depth + 1, last]
+    x_eta = beside_x(1, eta_send_low, eta_send_high, eta_low, eta_high)
+    z_eta = beside_z(1, eta.at[facing], eta.at[edge])
+    z_first.wait()
+    z_eta.wait()
 
     def start(z):
         return fields[3, z + 1]
 
-    eta_low, eta_high = get_low.at[4], get_high.at[4]
-    exchange(0, fields, 5, send_low, send_high, get_low, get_high)
-
     def first(z, carry):
-        values = new_plane(
-            z, fields, eta, get_low, get_high, eta_low, eta_high, density, inverse, start
-        )
+        values = inner_planes(z, fields, eta, density, inverse, start)
         for f in range(4):
             middle[f, z + 1] = values[f]
         return carry
 
     lax.fori_loop(0, depth, first, 0)
-    exchange(1, middle, 4, send_low2, send_high2, get_low2, get_high2)
+    wait_x(x_first)
+    wait_x(x_eta)
+    for row, halo, eta_halo, out in (
+        (0, get_low, eta_low, send_low2), (last, get_high, eta_high, send_high2)
+    ):
+        values = edge_rows(row, fields, eta, halo, eta_halo, density, inverse, fields)
+        for f in range(4):
+            out[f] = values[f]
+    x_second = beside_x(2, send_low2, send_high2, get_low2, get_high2)
+    for f in range(4):
+        middle[f, 1 : depth + 1, 0] = send_low2[f]
+        middle[f, 1 : depth + 1, last] = send_high2[f]
+    beside_z(2, middle.at[:, facing], middle.at[:, edge]).wait()
 
     def second(z, carry):
-        values = new_plane(
-            z, middle, eta, get_low2, get_high2, eta_low, eta_high, density, inverse, start
-        )
+        values = inner_planes(z, middle, eta, density, inverse, start)
         for f in range(4):
             result[f, z] = values[f]
         loaded[z] = density[z] * (1.0 + squeeze * values[3])
         return carry
 
     lax.fori_loop(0, depth, second, 0)
-    outs = [
-        pltpu.make_async_copy(result.at[pl.ds(0, 3)], velocity_out, out_sem.at[0]),
-        pltpu.make_async_copy(result.at[3], pressure_out, out_sem.at[1]),
-    ]
-    for copy in outs:
-        copy.start()
-
-    loads[3].wait()
-    loads[4].wait()
-    high, low = split_value(loaded[...].reshape(depth * width, lateral))
-    both = dot(jnp.concatenate([high, low], axis=0), ty_high[...])
-    rows = both[: depth * width] + both[depth * width :] + dot(high, ty_low[...])
 
     index_x = lax.broadcasted_iota(jnp.int32, (total_x, HALF_MODES), 0)
-    index_y = lax.broadcasted_iota(jnp.int32, (total_x, HALF_MODES), 1)
+    index_y = mode_at(lax.broadcasted_iota(jnp.int32, (total_x, HALF_MODES), 1), ranks)
     wx, wy = wave_of(index_x, total_x), wave_of(index_y, NY)
     magnitude = jnp.sqrt(wx * wx + wy * wy)
     decay = jnp.exp(-layer_depth * magnitude)
+    above = jnp.exp(-(layer_depth * depth) * magnitude * gz.astype(jnp.float32))
+    for copy in loads[3:]:
+        copy.wait()
+
+    wait_x(x_second)
+    for row, halo, eta_halo in ((0, get_low2, eta_low), (last, get_high2, eta_high)):
+        values = edge_rows(row, middle, eta, halo, eta_halo, density, inverse, fields)
+        for f in range(4):
+            result[f, :, row] = values[f]
+        loaded[:, row] = density[:, row] * (1.0 + squeeze * values[3])
+
+    high, low = split_value(loaded[...].reshape(depth * width, lateral))
+    both = dot(jnp.concatenate([high, low], axis=0), ty[0])
+    rows = both[: depth * width] + both[depth * width :] + dot(high, ty[1])
     decay = jnp.concatenate([decay, decay], axis=0)
     weights = along_x[...]
     total = None
@@ -498,81 +544,91 @@
         high, low = split_value(layer)
         spectrum = dot(weights, jnp.concatenate([high, low, high], axis=0))
         total = spectrum if total is None else total * decay + spectrum
-    above = jnp.exp(-(layer_depth * depth) * magnitude * gz.astype(jnp.float32))
     real = jnp.transpose(total[:total_x] * above)
     imag = jnp.transpose(total[total_x:] * above)
     cos_row, sin_row = phase[0, pl.ds(gx, 1), :], phase[1, pl.ds(gx, 1), :]
-    partial[:, :total_x] = real * cos_row + imag * sin_row
-    partial[:, total_x:] = imag * cos_row - real * sin_row
-
-    held = HALF_MODES // layers
+    shape = (2, ranks, 8, total_x)
+    partial[:, :, :, :total_x] = (real * cos_row + imag * sin_row).reshape(shape)
+    partial[:, :, :, total_x:] = (imag * cos_row - real * sin_row).reshape(shape)
+
     across = pltpu.make_async_remote_copy(
-        src_ref=partial.at[pl.ds(pl.multiple_of(held * (1 - gz), held), held)],
+        src_ref=partial.at[:, pl.ds(groups * (1 - gz), groups)],
         dst_ref=got_z,
         send_sem=pair_sem.at[0], recv_sem=pair_sem.at[1],
         device_id=(model, gx, 1 - gz), device_id_type=MESH,
     )
     across.start()
     across.wait()
-    own = held // groups
-    mine[...] = partial[pl.ds(pl.multiple_of(held * gz, held), held)] + got_z[...]
+    mine[...] = partial[:, pl.ds(groups * gz, groups)] + got_z[...]
 
     copies = []
     for j in range(1, groups):
         target = lax.rem(gx + j, groups)
         copy = pltpu.make_async_remote_copy(
-            src_ref=mine.at[pl.ds(pl.multiple_of(target * own, own), own)],
+            src_ref=mine.at[:, target],
             dst_ref=got_x.at[gx],
             send_sem=send_sem.at[j], recv_sem=recv_sem.at[j],
             device_id=(model, target, gz), device_id_type=MESH,
         )
         copy.start()
         copies.append(copy)
-    index_x = lax.broadcasted_iota(jnp.int32, (own, total_x), 1)
-    index_y = lax.broadcasted_iota(jnp.int32, (own, total_x), 0) + (held * gz + own * gx)
+    slot = gz * groups + gx
+    index_x = lax.broadcasted_iota(jnp.int32, (16, total_x), 1)
+    index_y = lax.broadcasted_iota(jnp.int32, (16, total_x), 0) + 16 * slot
     wx, wy = wave_of(index_x, total_x), wave_of(index_y, NY)
     scale = gravity_scale * layer_depth / (total_x * NY)
     weight = scale * jnp.exp((-0.5 * layer_depth) * jnp.sqrt(wx * wx + wy * wy))
     weight = weight * jnp.where(index_y == 0, jnp.where(index_x == 0, 0.0, 1.0), 2.0)
     weight = jnp.concatenate([weight, weight], axis=1)
-    summed = mine[pl.ds(pl.multiple_of(gx * own, own), own)]
+    summed = mine[:, gx]
     for j in range(1, groups):
         copies[j - 1].wait_recv()
         summed = summed + got_x[lax.rem(gx + groups - j, groups)]
-    loads[5].wait()
-    loads[6].wait()
-    high, low = split_value(summed * weight)
-    both = dot(jnp.concatenate([high, low], axis=0), bx_high[...])
-    columns = both[:own] + both[own:] + dot(high, bx_low[...])
-    for part in range(2 * total_x // 128):
-        back[part] = columns[:, 128 * part : 128 * (part + 1)]
-
-    per_part = 128 // (2 * width)
-    slot = gz * groups + gx
+    high, low = split_value(summed.reshape(16, 2 * total_x) * weight)
+    both = dot(jnp.concatenate([high, low], axis=0), bx[0])
+    columns = both[:16] + both[16:] + dot(high, bx[1])
+
+    lane = lax.broadcasted_iota(jnp.int32, (8, 128), 1)
+    span = 2 * width
+    for target in range(groups):
+        place = span * target
+        group, offset = place // 128 * 128, place % 128
+        upper = pltpu.roll(columns[:8, group : group + 128], (128 - offset) % 128, 1)
+        lower = pltpu.roll(columns[8:, group : group + 128], (128 + span - offset) % 128, 1)
+        back[target] = jnp.where(lane < span, upper, lower)
     returns = []
     for j in range(1, ranks):
         other = lax.rem(rank + j, ranks)
         copy = pltpu.make_async_remote_copy(
-            src_ref=back.at[(other // layers) // per_part],
+            src_ref=back.at[other // layers],
             dst_ref=got_back.at[slot],
             send_sem=send_sem2.at[j], recv_sem=recv_sem2.at[j],
             device_id=(model, other // layers, lax.rem(other, layers)), device_id_type=MESH,
         )
         copy.start()
         returns.append(copy)
-    got_back[slot] = back[gx // per_part]
+    got_back[slot] = back[gx]
     for copy in returns:
         copy.wait_recv()
-    waves = got_back[...].reshape(HALF_MODES, 128)
-    waves = pltpu.roll(waves, lax.rem(128 - 2 * width * lax.rem(gx, per_part), 128), 1)
-    waves = jnp.transpose(waves)
-    waves = jnp.concatenate([waves[:width], waves[width : 2 * width]], axis=1)
-    high, low = split_value(waves)
-    both = dot_turned(jnp.concatenate([high, low], axis=0), ty_high[...])
-    gravity[...] = both[:width] + both[width:] + dot_turned(high, ty_low[...])
-
+    waves = jnp.transpose(got_back[...].reshape(8 * ranks, 128))
+    waves_out[...] = jnp.concatenate(
+        [waves[i * width : (i + 1) * width] for i in (0, 2, 1, 3)], axis=1
+    )
     for copy in copies + returns:
         copy.wait_send()
+
+
+def last_kernel(result, waves, ty, velocity_out, pressure_out, gravity, sem):
+    outs = [
+        pltpu.make_async_copy(result.at[pl.ds(0, 3)], velocity_out, sem.at[0]),
+        pltpu.make_async_copy(result.at[3], pressure_out, sem.at[1]),
+    ]
+    for copy in outs:
+        copy.start()
+    width = waves.shape[0]
+    high, low = split_value(waves[...])
+    both = dot_turned(jnp.concatenate([high, low], axis=0), ty[0])
+    gravity[...] = both[:width] + both[width:] + dot_turned(high, ty[1])
     for copy in outs:
         copy.wait()
 
@@ -581,56 +637,68 @@
     depth, width, lateral = pressure.shape
     groups, layers = lax.axis_size("gx"), lax.axis_size("gz")
     total_x = groups * width
-    ty, along_x, phase, bx = host_tables(groups, width, total_x)
-    held = HALF_MODES // layers
-    own = held // groups
+    ty, along_x, phase, bx = host_tables(groups, layers, width, total_x)
     ranks = groups * layers
     f32, b16 = jnp.float32, jnp.bfloat16
     vmem = pl.BlockSpec(memory_space=pltpu.VMEM)
     smem = pl.BlockSpec(memory_space=pltpu.SMEM)
     anywhere = pl.BlockSpec(memory_space=pl.ANY)
-    rows5, rows4 = pltpu.VMEM((5, depth, lateral), f32), pltpu.VMEM((4, depth, lateral), f32)
+    hbm = pl.BlockSpec(memory_space=pltpu.HBM)
+    rows = pltpu.VMEM((4, depth, lateral), f32)
+    eta_rows = pltpu.VMEM((depth, lateral), f32)
     cells = (depth, width, lateral)
     sems = pltpu.SemaphoreType.DMA
+    along_y = jnp.asarray(ty)
+    result, waves = pl.pallas_call(
+        functools.partial(kernel, groups, layers),
+        out_shape=(
+            pltpu.VMEM((4,) + cells, f32),
+            pltpu.VMEM((width, 2 * HALF_MODES), f32),
+        ),
+        in_specs=[smem, smem] + [hbm] * 7,
+        out_specs=(vmem, vmem),
+        scratch_shapes=[
+            pltpu.VMEM(cells, jnp.int32),
+            pltpu.VMEM((4, depth + 2, width, lateral), f32),
+            pltpu.VMEM((depth + 2, width, lateral), f32),
+            pltpu.VMEM((4, depth + 2, width, lateral), f32),
+            pltpu.VMEM(cells, f32),
+            pltpu.VMEM(cells, f32),
+            rows, rows, rows, rows, rows, rows, rows, rows,
+            eta_rows, eta_rows, eta_rows, eta_rows,
+            pltpu.VMEM(ty.shape, b16),
+            pltpu.VMEM(along_x.shape, b16),
+            pltpu.VMEM(phase.shape, f32),
+            pltpu.VMEM(bx.shape, b16),
+            pltpu.VMEM(cells, f32),
+            pltpu.VMEM((2, ranks, 8, 2 * total_x), f32),
+            pltpu.VMEM((2, groups, 8, 2 * total_x), f32),
+            pltpu.VMEM((2, groups, 8, 2 * total_x), f32),
+            pltpu.VMEM((groups, 2, 8, 2 * total_x), f32),
+            pltpu.VMEM((groups, 8, 128), f32),
+            pltpu.VMEM((ranks, 8, 128), f32),
+            sems((7,)), sems((6,)), sems((12,)), sems((2,)),
+            sems((groups,)), sems((groups,)), sems((ranks,)), sems((ranks,)),
+        ],
+        compiler_params=pltpu.CompilerParams(
+            collective_id=0, has_side_effects=True, vmem_limit_bytes=56 * 1024 * 1024
+        ),
+    )(
+        density_table, viscosity_table, phases, velocity, pressure,
+        along_y, jnp.asarray(along_x), jnp.asarray(phase), jnp.asarray(bx),
+    )
     return pl.pallas_call(
-        functools.partial(kernel, groups, layers),
+        last_kernel,
         out_shape=(
             jax.ShapeDtypeStruct(velocity.shape, f32),
             jax.ShapeDtypeStruct(pressure.shape, f32),
             jax.ShapeDtypeStruct((width, lateral), f32),
         ),
-        in_specs=[smem, smem] + [anywhere] * 5 + [vmem] * 2 + [anywhere] * 2,
-        out_specs=(anywhere, anywhere, vmem),
-        scratch_shapes=[
-            pltpu.VMEM(cells, jnp.int32),
-            pltpu.VMEM((5, depth + 2, width, lateral), f32),
-            pltpu.VMEM((4, depth + 2, width, lateral), f32),
-            pltpu.VMEM((4,) + cells, f32),
-            pltpu.VMEM(cells, f32),
-            pltpu.VMEM(cells, f32),
-            rows5, rows5, rows5, rows5, rows4, rows4, rows4, rows4,
-            pltpu.VMEM(ty[0].shape, b16),
-            pltpu.VMEM(ty[0].shape, b16),
-            pltpu.VMEM(bx[0].shape, b16),
-            pltpu.VMEM(bx[0].shape, b16),
-            pltpu.VMEM(cells, f32),
-            pltpu.VMEM((HALF_MODES, 2 * total_x), f32),
-            pltpu.VMEM((held, 2 * total_x), f32),
-            pltpu.VMEM((held, 2 * total_x), f32),
-            pltpu.VMEM((groups, own, 2 * total_x), f32),
-            pltpu.VMEM((2 * total_x // 128, own, 128), f32),
-            pltpu.VMEM((ranks, own, 128), f32),
-            sems((7,)), sems((4,)), sems((8,)), sems((2,)), sems((2,)),
-            sems((groups,)), sems((groups,)), sems((ranks,)), sems((ranks,)),
-        ],
-        compiler_params=pltpu.CompilerParams(
-            collective_id=0, has_side_effects=True, vmem_limit_bytes=40 * 1024 * 1024
-        ),
-    )(
-        density_table, viscosity_table, phases, velocity, pressure,
-        jnp.asarray(ty[0]), jnp.asarray(ty[1]), jnp.asarray(along_x), jnp.asarray(phase),
-        jnp.asarray(bx[0]), jnp.asarray(bx[1]),
-    )
+        in_specs=[vmem] * 3,
+        out_specs=(hbm, hbm, vmem),
+        scratch_shapes=[sems((2,))],
+        compiler_params=pltpu.CompilerParams(vmem_limit_bytes=16 * 1024 * 1024),
+    )(result, waves, along_y)
 
 
 def local_program(phases, velocity, pressure, density_table, viscosity_table):

time: 46.1 us -> 32.4 us (0.70)
  local copies, waits for them, and re-layouts: 12 us -> 0.01 us
  Pallas kernels: 33 us -> 31.5 us
    unnamed x25 -> x2, local copies, waits for them, and re-layouts: 12 us -> 0.01 us
    pallas_call x1 -> x2, Pallas kernels: 33 us -> 31.5 us  [the longest x1 29.9 us: fused_body(): pl.pallas_call(functools.partial(kernel, groups, layers), out_shape=(pltp...]
where the time goes in v1:
time: 32.4 us; the launch traced here: 32.2 us
  Pallas kernels  31.5 us (97%)
  between operations  0.66 us (2%)
    pallas_call x1, Pallas kernels, fused_body(): pl.pallas_call(functools.partial(kernel, groups, layers), out_shape=(pltp...  29.9 us
    pallas_call x1, Pallas kernels, fused_body(): pl.pallas_call(last_kernel, out_shape=(jax.ShapeDtypeStruct(velocity.shap...  1.66 us

profile of v1, /device:TPU:0, one launch (start us, length us, event | category | flops | bytes accessed | tf_op | source)
XLA Modules:
  0.0 32.2 jit_solution(17335869521298909874)
XLA Ops:
  0.6 0.0 copy-start
  0.6 29.9 %shard_map.112 = (f32[4,8,16,512]{3,2,1,0:T(8,128)S(1)}, f32[16,512]{1,0:T(8,128)S(1)}) custom-call(f32[8]{0:T(128)} %dens_ref.1, f32[8]{0:T(128)} %visc_ref.1, s32[8,16,512]{2,1,0:T(8,128)} %phases_hbm.1, f32[3,8,16,512]{3,2,1,0:T(8,128)} %velocity_hbm.1, f32[8,16,512]{2,1,0:T(8,128)} %pressure_hbm.1, bf16[2,512,512]{2,1,0:T(8,128)(2,1)} %constant.8.clone.ty_hbm.ty, ...), custom_call_target="tpu_custom_call" | custom-call | tf_op jit(solution)/shard_map/pallas_call | solution.py:652
  30.5 0.0 copy-done
  30.5 1.7 %shard_map.113 = (f32[3,8,16,512]{3,2,1,0:T(8,128)}, f32[8,16,512]{2,1,0:T(8,128)}, f32[16,512]{1,0:T(8,128)}) custom-call(f32[4,8,16,512]{3,2,1,0:T(8,128)S(1)} %get-tuple-element.5.result, f32[16,512]{1,0:T(8,128)S(1)} %get-tuple-element.6.waves, bf16[2,512,512]{2,1,0:T(8,128)(2,1)S(1)} %copy-done), custom_call_target="tpu_custom_call" | custom-call | tf_op jit(solution)/shard_map/pallas_call | solution.py:690
Async XLA Ops:
  0.6 29.9 %copy-start = (bf16[2,512,512]{2,1,0:T(8,128)(2,1)S(1)}, bf16[2,512,512]{2,1,0:T(8,128)(2,1)}, u32[]{:S(2)}) copy-start(bf16[2,512,512]{2,1,0:T(8,128)(2,1)} %constant.8.clone.ty_hbm.ty) | copy-start | bytes 3145732

commit v2 on v1

--- a/solution.py
+++ b/solution.py
@@ -268,26 +268,18 @@
     return shifted.astype(jnp.float32) * (2.0 * math.pi / length)
 
 
-def advance(values, sides, faces, density, inverse, start):
-    total_face = sum(faces[1:], faces[0])
-    rate = (0.5 * velocity_rate) * inverse
-    results = []
-    spread = None
-    for f in range(3):
-        flux = faces[0] * sides[f][0]
-        for n in range(1, 6):
-            flux = flux + faces[n] * sides[f][n]
-        forcing = flux - total_face * values[f]
-        forcing = forcing - (sides[3][2 * f] - sides[3][2 * f + 1])
-        if f == 2:
-            forcing = forcing - 2.0 * density
-        results.append(values[f] + rate * forcing)
-        change = sides[f][2 * f] - sides[f][2 * f + 1]
-        spread = change if spread is None else spread + change
-    results.append(
-        values[3] - pressure_rate * (0.5 * spread + (values[3] - start) / bulk_time)
-    )
-    return results
+def new_velocity(f, value, side, faces, gradient, density, inverse):
+    flux = faces[0] * side[0]
+    for n in range(1, 6):
+        flux = flux + faces[n] * side[n]
+    forcing = flux - sum(faces[1:], faces[0]) * value - gradient
+    if f == 2:
+        forcing = forcing - 2.0 * density
+    return value + (0.5 * velocity_rate) * inverse * forcing
+
+
+def new_pressure(value, spread, start):
+    return value - pressure_rate * (0.5 * spread + (value - start) / bulk_time)
 
 
 def beside_y(tile):
@@ -299,49 +291,79 @@
     )
 
 
-def inner_planes(z, block, eta, density, inverse, start):
-    def around(ref, lead):
-        plane = ref[lead + (z + 1,)]
-        width = plane.shape[0]
-        ahead, behind = beside_y(plane)
-        return plane, (
-            pltpu.roll(plane, width - 1, 0), pltpu.roll(plane, 1, 0), ahead, behind,
-            ref[lead + (z + 2,)], ref[lead + (z,)],
-        )
-
-    center, others = around(eta, ())
+def beside_plane(ref, lead, z):
+    plane = ref[lead + (z + 1,)]
+    width = plane.shape[0]
+    ahead, behind = beside_y(plane)
+    return plane, (
+        pltpu.roll(plane, width - 1, 0), pltpu.roll(plane, 1, 0), ahead, behind,
+        ref[lead + (z + 2,)], ref[lead + (z,)],
+    )
+
+
+def inner_velocity(z, block, eta, density, inverse):
+    center, others = beside_plane(eta, (), z)
     faces = [center + other for other in others]
-    pairs = [around(block, (f,)) for f in range(4)]
-    return advance(
-        [p[0] for p in pairs], [p[1] for p in pairs], faces, density[z], inverse[z], start(z)
-    )
-
-
-def edge_rows(row, block, eta, halo, eta_halo, density, inverse, first):
-    depth = density.shape[0]
-    inward = 1 if row == 0 else -1
-
-    def around(ref, lead, outer):
-        tile = ref[lead + (slice(1, depth + 1), row)]
-        layer = lax.broadcasted_iota(jnp.int32, tile.shape, 0)
-        below = jnp.where(layer == 0, ref[lead + (slice(0, 1), row)], pltpu.roll(tile, 1, 0))
-        above = jnp.where(
-            layer == depth - 1,
-            ref[lead + (slice(depth + 1, depth + 2), row)],
-            pltpu.roll(tile, depth - 1, 0),
-        )
-        ahead, behind = beside_y(tile)
-        inner = ref[lead + (slice(1, depth + 1), row + inward)]
-        along = (inner, outer) if row == 0 else (outer, inner)
-        return tile, along + (ahead, behind, above, below)
-
-    center, others = around(eta, (), eta_halo[...])
+    pairs = [beside_plane(block, (f,), z) for f in range(4)]
+    push = pairs[3][1]
+    return [
+        new_velocity(
+            f, pairs[f][0], pairs[f][1], faces, push[2 * f] - push[2 * f + 1], density[z], inverse[z]
+        )
+        for f in range(3)
+    ]
+
+
+def inner_pressure(z, block, start):
+    width = block.shape[2]
+    along_x, along_y = block[0, z + 1], block[1, z + 1]
+    ahead, behind = beside_y(along_y)
+    spread = pltpu.roll(along_x, width - 1, 0) - pltpu.roll(along_x, 1, 0)
+    spread = spread + (ahead - behind) + (block[2, z + 2] - block[2, z])
+    return new_pressure(block[3, z + 1], spread, start[3, z + 1])
+
+
+def beside_row(ref, lead, row, outer):
+    depth = ref.shape[-3] - 2
+    tile = ref[lead + (slice(1, depth + 1), row)]
+    layer = lax.broadcasted_iota(jnp.int32, tile.shape, 0)
+    below = jnp.where(layer == 0, ref[lead + (slice(0, 1), row)], pltpu.roll(tile, 1, 0))
+    above = jnp.where(
+        layer == depth - 1,
+        ref[lead + (slice(depth + 1, depth + 2), row)],
+        pltpu.roll(tile, depth - 1, 0),
+    )
+    ahead, behind = beside_y(tile)
+    inner = ref[lead + (slice(1, depth + 1), row + 1 if row == 0 else row - 1)]
+    along = (inner, outer) if row == 0 else (outer, inner)
+    return tile, along + (ahead, behind, above, below)
+
+
+def edge_velocity(wanted, row, block, eta, halo, eta_halo, density, inverse):
+    center, others = beside_row(eta, (), row, eta_halo[...])
     faces = [center + other for other in others]
-    pairs = [around(block, (f,), halo[f]) for f in range(4)]
-    return advance(
-        [p[0] for p in pairs], [p[1] for p in pairs], faces,
-        density[:, row], inverse[:, row], first[3, 1 : depth + 1, row],
-    )
+    push = beside_row(block, (3,), row, halo[3])[1]
+    results = []
+    for f in wanted:
+        value, side = beside_row(block, (f,), row, halo[f])
+        results.append(
+            new_velocity(
+                f, value, side, faces, push[2 * f] - push[2 * f + 1], density[:, row],
+                inverse[:, row],
+            )
+        )
+    return results
+
+
+def edge_pressure(row, block, halo, start):
+    depth = block.shape[1] - 2
+    spread = None
+    for f in range(3):
+        side = beside_row(block, (f,), row, halo[f])[1]
+        change = side[2 * f] - side[2 * f + 1]
+        spread = change if spread is None else spread + change
+    here = slice(1, depth + 1)
+    return new_pressure(block[3, here, row], spread, start[3, here, row])
 
 
 def kernel(
@@ -377,7 +399,7 @@
             ]
         )
     ]
-    for copy in loads:
+    for copy in loads[:3]:
         copy.start()
 
     barrier = pltpu.get_barrier_semaphore()
@@ -416,29 +438,43 @@
             send_sem=x_sem.at[4 * stage + 2], recv_sem=x_sem.at[4 * stage + 3],
             device_id=(model, lax.rem(gx + 1, groups), gz), device_id_type=MESH,
         )
-
+        return down, up
+
+    def send(pairs, rows=(0, last)):
+        if 0 in rows:
+            @pl.when(gx > 0)
+            def _():
+                for down, up in pairs:
+                    down.start()
+
+        if last in rows:
+            @pl.when(gx < groups - 1)
+            def _():
+                for down, up in pairs:
+                    up.start()
+
+    def receive(pairs, row):
+        if row == 0:
+            @pl.when(gx > 0)
+            def _():
+                for down, up in pairs:
+                    up.wait_recv()
+        else:
+            @pl.when(gx < groups - 1)
+            def _():
+                for down, up in pairs:
+                    down.wait_recv()
+
+    def all_sent(pairs):
         @pl.when(gx > 0)
         def _():
-            down.start()
+            for down, up in pairs:
+                down.wait_send()
 
         @pl.when(gx < groups - 1)
         def _():
-            up.start()
-
-        return down, up
-
-    def wait_x(pair):
-        down, up = pair
-
-        @pl.when(gx > 0)
-        def _():
-            down.wait_send()
-            up.wait_recv()
-
-        @pl.when(gx < groups - 1)
-        def _():
-            up.wait_send()
-            down.wait_recv()
+            for down, up in pairs:
+                up.wait_send()
 
     def beside_z(stage, source, target):
         copy = pltpu.make_async_remote_copy(
@@ -448,6 +484,19 @@
         )
         copy.start()
         return copy
+
+    bundle = (send_low, send_high, get_low, get_high)
+    bundle2 = (send_low2, send_high2, get_low2, get_high2)
+    x_u = beside_x(0, *[ref.at[0] for ref in bundle])
+    x_p = beside_x(1, *[ref.at[3] for ref in bundle])
+    x_eta = beside_x(2, eta_send_low, eta_send_high, eta_low, eta_high)
+    x_rest = beside_x(3, *[ref.at[pl.ds(1, 2)] for ref in bundle])
+    x_u2 = beside_x(4, *[ref.at[0] for ref in bundle2])
+    x_rest2 = beside_x(5, *[ref.at[pl.ds(1, 3)] for ref in bundle2])
+    edges = (
+        (0, get_low, eta_low, send_low2, get_low2),
+        (last, get_high, eta_high, send_high2, get_high2),
+    )
 
     facing = depth - (depth - 1) * gz
     loads[0].wait()
@@ -456,10 +505,12 @@
         send_low[f] = fields[f, 1 : depth + 1, 0]
         send_high[f] = fields[f, 1 : depth + 1, last]
     pl.semaphore_wait(barrier, ranks - 1)
-    x_first = beside_x(0, send_low, send_high, get_low, get_high)
+    send([x_u, x_p])
     z_first = beside_z(0, fields.at[:, facing], fields.at[:, edge])
 
     loads[2].wait()
+    for copy in loads[3:]:
+        copy.start()
 
     def look_up(z, carry):
         kind = ph[z]
@@ -478,40 +529,41 @@
     lax.fori_loop(0, depth, look_up, 0)
     eta_send_low[...] = eta[1 : depth + 1, 0]
     eta_send_high[...] = eta[1 : depth + 1, last]
-    x_eta = beside_x(1, eta_send_low, eta_send_high, eta_low, eta_high)
+    send([x_eta, x_rest])
     z_eta = beside_z(1, eta.at[facing], eta.at[edge])
     z_first.wait()
     z_eta.wait()
 
-    def start(z):
-        return fields[3, z + 1]
-
     def first(z, carry):
-        values = inner_planes(z, fields, eta, density, inverse, start)
+        values = inner_velocity(z, fields, eta, density, inverse)
+        for f in range(3):
+            middle[f, z + 1] = values[f]
+        middle[3, z + 1] = inner_pressure(z, fields, fields)
+        return carry
+
+    lax.fori_loop(0, depth, first, 0)
+
+    for row, halo, eta_halo, out, later in edges:
+        receive([x_u, x_p, x_eta], row)
+        out[0] = edge_velocity((0,), row, fields, eta, halo, eta_halo, density, inverse)[0]
+        send([x_u2], (row,))
+    for row, halo, eta_halo, out, later in edges:
+        receive([x_rest], row)
+        out[1], out[2] = edge_velocity(
+            (1, 2), row, fields, eta, halo, eta_halo, density, inverse
+        )
+        out[3] = edge_pressure(row, fields, halo, fields)
+    for row, halo, eta_halo, out, later in edges:
         for f in range(4):
-            middle[f, z + 1] = values[f]
-        return carry
-
-    lax.fori_loop(0, depth, first, 0)
-    wait_x(x_first)
-    wait_x(x_eta)
-    for row, halo, eta_halo, out in (
-        (0, get_low, eta_low, send_low2), (last, get_high, eta_high, send_high2)
-    ):
-        values = edge_rows(row, fields, eta, halo, eta_halo, density, inverse, fields)
-        for f in range(4):
-            out[f] = values[f]
-    x_second = beside_x(2, send_low2, send_high2, get_low2, get_high2)
-    for f in range(4):
-        middle[f, 1 : depth + 1, 0] = send_low2[f]
-        middle[f, 1 : depth + 1, last] = send_high2[f]
-    beside_z(2, middle.at[:, facing], middle.at[:, edge]).wait()
+            middle[f, 1 : depth + 1, row] = out[f]
+    z_second = beside_z(2, middle.at[:, facing], middle.at[:, edge])
+    send([x_rest2])
+    z_second.wait()
 
     def second(z, carry):
-        values = inner_planes(z, middle, eta, density, inverse, start)
-        for f in range(4):
-            result[f, z] = values[f]
-        loaded[z] = density[z] * (1.0 + squeeze * values[3])
+        pressure = inner_pressure(z, middle, fields)
+        result[3, z] = pressure
+        loaded[z] = density[z] * (1.0 + squeeze * pressure)
         return carry
 
     lax.fori_loop(0, depth, second, 0)
@@ -524,13 +576,11 @@
     above = jnp.exp(-(layer_depth * depth) * magnitude * gz.astype(jnp.float32))
     for copy in loads[3:]:
         copy.wait()
-
-    wait_x(x_second)
-    for row, halo, eta_halo in ((0, get_low2, eta_low), (last, get_high2, eta_high)):
-        values = edge_rows(row, middle, eta, halo, eta_halo, density, inverse, fields)
-        for f in range(4):
-            result[f, :, row] = values[f]
-        loaded[:, row] = density[:, row] * (1.0 + squeeze * values[3])
+    for row, halo, eta_halo, out, later in edges:
+        receive([x_u2], row)
+        pressure = edge_pressure(row, middle, later, fields)
+        result[3, :, row] = pressure
+        loaded[:, row] = density[:, row] * (1.0 + squeeze * pressure)
 
     high, low = split_value(loaded[...].reshape(depth * width, lateral))
     both = dot(jnp.concatenate([high, low], axis=0), ty[0])
@@ -562,7 +612,8 @@
     mine[...] = partial[:, pl.ds(groups * gz, groups)] + got_z[...]
 
     copies = []
-    for j in range(1, groups):
+    distant = sorted(range(1, groups), key=lambda j: -min(j, groups - j))
+    for j in distant:
         target = lax.rem(gx + j, groups)
         copy = pltpu.make_async_remote_copy(
             src_ref=mine.at[:, target],
@@ -572,6 +623,20 @@
         )
         copy.start()
         copies.append(copy)
+    def third(z, carry):
+        values = inner_velocity(z, middle, eta, density, inverse)
+        for f in range(3):
+            result[f, z] = values[f]
+        return carry
+
+    lax.fori_loop(0, depth, third, 0)
+    for row, halo, eta_halo, out, later in edges:
+        receive([x_rest2], row)
+        values = edge_velocity((0, 1, 2), row, middle, eta, later, eta_halo, density, inverse)
+        for f in range(3):
+            result[f, :, row] = values[f]
+    all_sent([x_u, x_p, x_eta, x_rest, x_u2, x_rest2])
+
     slot = gz * groups + gx
     index_x = lax.broadcasted_iota(jnp.int32, (16, total_x), 1)
     index_y = lax.broadcasted_iota(jnp.int32, (16, total_x), 0) + 16 * slot
@@ -581,8 +646,8 @@
     weight = weight * jnp.where(index_y == 0, jnp.where(index_x == 0, 0.0, 1.0), 2.0)
     weight = jnp.concatenate([weight, weight], axis=1)
     summed = mine[:, gx]
-    for j in range(1, groups):
-        copies[j - 1].wait_recv()
+    for j, copy in zip(distant, copies):
+        copy.wait_recv()
         summed = summed + got_x[lax.rem(gx + groups - j, groups)]
     high, low = split_value(summed.reshape(16, 2 * total_x) * weight)
     both = dot(jnp.concatenate([high, low], axis=0), bx[0])
@@ -597,7 +662,7 @@
         lower = pltpu.roll(columns[8:, group : group + 128], (128 + span - offset) % 128, 1)
         back[target] = jnp.where(lane < span, upper, lower)
     returns = []
-    for j in range(1, ranks):
+    for j in sorted(range(1, ranks), key=lambda j: -min(j, ranks - j)):
         other = lax.rem(rank + j, ranks)
         copy = pltpu.make_async_remote_copy(
             src_ref=back.at[other // layers],
@@ -677,7 +742,7 @@
             pltpu.VMEM((groups, 2, 8, 2 * total_x), f32),
             pltpu.VMEM((groups, 8, 128), f32),
             pltpu.VMEM((ranks, 8, 128), f32),
-            sems((7,)), sems((6,)), sems((12,)), sems((2,)),
+            sems((7,)), sems((6,)), sems((24,)), sems((2,)),
             sems((groups,)), sems((groups,)), sems((ranks,)), sems((ranks,)),
         ],
         compiler_params=pltpu.CompilerParams(

time: 32.4 us -> 31 us (0.957)
  Pallas kernels: 31.5 us -> 30.2 us
    pallas_call x1, Pallas kernels: 29.9 us -> 28.5 us  [fused_body(): pl.pallas_call(functools.partial(kernel, groups, layers), out_shape=(pltp...]
where the time goes in v2:
time: 31 us; the launch traced here: 30.8 us
  Pallas kernels  30.2 us (97%)
  between operations  0.66 us (2%)
    pallas_call x1, Pallas kernels, fused_body(): pl.pallas_call(functools.partial(kernel, groups, layers), out_shape=(pltp...  28.5 us
    pallas_call x1, Pallas kernels, fused_body(): pl.pallas_call(last_kernel, out_shape=(jax.ShapeDtypeStruct(velocity.shap...  1.66 us

profile of v2, /device:TPU:0, one launch (start us, length us, event | category | flops | bytes accessed | tf_op | source)
XLA Modules:
  0.0 30.8 jit_solution(3402125321096850606)
XLA Ops:
  0.6 0.0 copy-start
  0.6 28.5 %shard_map.112 = (f32[4,8,16,512]{3,2,1,0:T(8,128)S(1)}, f32[16,512]{1,0:T(8,128)S(1)}) custom-call(f32[8]{0:T(128)} %dens_ref.1, f32[8]{0:T(128)} %visc_ref.1, s32[8,16,512]{2,1,0:T(8,128)} %phases_hbm.1, f32[3,8,16,512]{3,2,1,0:T(8,128)} %velocity_hbm.1, f32[8,16,512]{2,1,0:T(8,128)} %pressure_hbm.1, bf16[2,512,512]{2,1,0:T(8,128)(2,1)} %constant.8.clone.ty_hbm.ty, ...), custom_call_target="tpu_custom_call" | custom-call | tf_op jit(solution)/shard_map/pallas_call | solution.py:717
  29.1 0.0 copy-done
  29.2 1.7 %shard_map.113 = (f32[3,8,16,512]{3,2,1,0:T(8,128)}, f32[8,16,512]{2,1,0:T(8,128)}, f32[16,512]{1,0:T(8,128)}) custom-call(f32[4,8,16,512]{3,2,1,0:T(8,128)S(1)} %get-tuple-element.5.result, f32[16,512]{1,0:T(8,128)S(1)} %get-tuple-element.6.waves, bf16[2,512,512]{2,1,0:T(8,128)(2,1)S(1)} %copy-done), custom_call_target="tpu_custom_call" | custom-call | tf_op jit(solution)/shard_map/pallas_call | solution.py:755
Async XLA Ops:
  0.6 28.5 %copy-start = (bf16[2,512,512]{2,1,0:T(8,128)(2,1)S(1)}, bf16[2,512,512]{2,1,0:T(8,128)(2,1)}, u32[]{:S(2)}) copy-start(bf16[2,512,512]{2,1,0:T(8,128)(2,1)} %constant.8.clone.ty_hbm.ty) | copy-start | bytes 3145732

commit v3 on v2

--- a/solution.py
+++ b/solution.py
@@ -219,11 +219,13 @@
     return high, low
 
 
-def host_tables(groups, layers, width, total_x):
+def host_tables(layers, width, total_x):
     y = np.arange(NY)[:, None]
-    k = mode_at(np.arange(HALF_MODES), groups * layers)[None, :]
+    k = np.arange(HALF_MODES)[None, :]
     angle = (y * k % NY) * (2.0 * np.pi / NY)
-    along_y = np.concatenate([np.cos(angle), -np.sin(angle)], axis=1).astype(np.float32)
+    along_y = np.stack(
+        [part.reshape(NY, layers, -1) for part in (np.cos(angle), -np.sin(angle))], axis=2
+    ).reshape(NY, 2 * HALF_MODES).astype(np.float32)
     kx = np.arange(total_x)[:, None]
     local = np.arange(width)[None, :]
     angle = (kx * local % total_x) * (2.0 * np.pi / total_x)
@@ -231,20 +233,11 @@
     along_x = np.block([[c, s], [-s, c]]).astype(np.float32)
     high, low = split_table(along_x)
     along_x = np.concatenate([high, high, low], axis=1)
-    angle = (kx * np.arange(groups)[None, :] * width % total_x) * (2.0 * np.pi / total_x)
-    phase = np.stack([np.cos(angle).T, np.sin(angle).T]).astype(np.float32)
     x = np.arange(total_x)[None, :]
     angle = (kx * x % total_x) * (2.0 * np.pi / total_x)
-    c = np.cos(angle).reshape(total_x, groups, 1, width)
-    s = np.sin(angle).reshape(total_x, groups, 1, width)
-    back_x = np.concatenate(
-        [np.concatenate([c, s], axis=2), np.concatenate([-s, c], axis=2)], axis=0
-    ).reshape(2 * total_x, groups * 2 * width).astype(np.float32)
-    return np.stack(split_table(along_y)), along_x, phase, np.stack(split_table(back_x))
-
-
-def mode_at(place, owners):
-    return place % (8 * owners) // 8 * 16 + place // (8 * owners) * 8 + place % 8
+    c, s = np.cos(angle), np.sin(angle)
+    back_x = np.block([[c, -s], [s, c]]).astype(np.float32)
+    return np.stack(split_table(along_y)), along_x, np.stack(split_table(back_x))
 
 
 def split_value(value):
@@ -369,14 +362,14 @@
 def kernel(
     groups, layers,
     dens_ref, visc_ref, phases_hbm, velocity_hbm, pressure_hbm,
-    ty_hbm, along_x_hbm, phase_hbm, bx_hbm,
+    ty_hbm, along_x_hbm, bx_hbm,
     result, waves_out,
     ph, fields, eta, middle, density, inverse,
     send_low, send_high, get_low, get_high, send_low2, send_high2, get_low2, get_high2,
     eta_send_low, eta_send_high, eta_low, eta_high,
-    ty, along_x, phase, bx,
-    loaded, partial, got_z, mine, got_x, back, got_back,
-    load_sem, z_sem, x_sem, pair_sem, send_sem, recv_sem, send_sem2, recv_sem2,
+    ty, along_x, bx,
+    loaded, partial, got_z, mine, got_x, whole,
+    load_sem, z_sem, x_sem, pair_sem, send_sem, recv_sem,
 ):
     model, gx, gz = lax.axis_index("models"), lax.axis_index("gx"), lax.axis_index("gz")
     depth, width, lateral = density.shape
@@ -394,7 +387,6 @@
                 (phases_hbm, ph),
                 (ty_hbm, ty),
                 (along_x_hbm, along_x),
-                (phase_hbm, phase),
                 (bx_hbm, bx),
             ]
         )
@@ -569,11 +561,14 @@
     lax.fori_loop(0, depth, second, 0)
 
     index_x = lax.broadcasted_iota(jnp.int32, (total_x, HALF_MODES), 0)
-    index_y = mode_at(lax.broadcasted_iota(jnp.int32, (total_x, HALF_MODES), 1), ranks)
+    index_y = lax.broadcasted_iota(jnp.int32, (total_x, HALF_MODES), 1)
     wx, wy = wave_of(index_x, total_x), wave_of(index_y, NY)
     magnitude = jnp.sqrt(wx * wx + wy * wy)
     decay = jnp.exp(-layer_depth * magnitude)
-    above = jnp.exp(-(layer_depth * depth) * magnitude * gz.astype(jnp.float32))
+    top = layer_depth * (0.5 + depth * gz.astype(jnp.float32))
+    scale = gravity_scale * layer_depth / (total_x * NY)
+    weight = scale * jnp.exp(-top * magnitude)
+    weight = weight * jnp.where(index_y == 0, jnp.where(index_x == 0, 0.0, 1.0), 2.0)
     for copy in loads[3:]:
         copy.wait()
     for row, halo, eta_halo, out, later in edges:
@@ -585,44 +580,55 @@
     high, low = split_value(loaded[...].reshape(depth * width, lateral))
     both = dot(jnp.concatenate([high, low], axis=0), ty[0])
     rows = both[: depth * width] + both[depth * width :] + dot(high, ty[1])
+    held = HALF_MODES // layers
+    parts = [rows[:, held * i : held * (i + 1)] for i in range(2 * layers)]
+    real = jnp.concatenate(parts[0::2], axis=1)
+    imag = jnp.concatenate(parts[1::2], axis=1)
     decay = jnp.concatenate([decay, decay], axis=0)
     weights = along_x[...]
     total = None
     for z in range(depth - 1, -1, -1):
-        layer = rows[z * width : (z + 1) * width]
-        layer = jnp.concatenate([layer[:, :HALF_MODES], layer[:, HALF_MODES:]], axis=0)
+        here = slice(z * width, (z + 1) * width)
+        layer = jnp.concatenate([real[here], imag[here]], axis=0)
         high, low = split_value(layer)
         spectrum = dot(weights, jnp.concatenate([high, low, high], axis=0))
         total = spectrum if total is None else total * decay + spectrum
-    real = jnp.transpose(total[:total_x] * above)
-    imag = jnp.transpose(total[total_x:] * above)
-    cos_row, sin_row = phase[0, pl.ds(gx, 1), :], phase[1, pl.ds(gx, 1), :]
-    shape = (2, ranks, 8, total_x)
-    partial[:, :, :, :total_x] = (real * cos_row + imag * sin_row).reshape(shape)
-    partial[:, :, :, total_x:] = (imag * cos_row - real * sin_row).reshape(shape)
-
-    across = pltpu.make_async_remote_copy(
-        src_ref=partial.at[:, pl.ds(groups * (1 - gz), groups)],
-        dst_ref=got_z,
-        send_sem=pair_sem.at[0], recv_sem=pair_sem.at[1],
-        device_id=(model, gx, 1 - gz), device_id_type=MESH,
-    )
-    across.start()
-    across.wait()
-    mine[...] = partial[:, pl.ds(groups * gz, groups)] + got_z[...]
-
+
+    high, low = split_value(total * jnp.concatenate([weight, weight], axis=0))
+    both = dot(bx[0], jnp.concatenate([high, low], axis=1))
+    field = both[:, :HALF_MODES] + both[:, HALF_MODES:] + dot(bx[1], high)
+    for i in range(layers):
+        partial[i] = field[:, held * i : held * (i + 1)].reshape(2, groups, width, held)
+
+    near = groups // 4
+    spans = [(near, groups - 2 * near), (0, near), (groups - near, near)]
+    across = []
+    for i, (begin, count) in enumerate(spans):
+        block = pl.ds(begin, count)
+        copy = pltpu.make_async_remote_copy(
+            src_ref=partial.at[1 - gz, :, block],
+            dst_ref=got_z.at[:, block],
+            send_sem=pair_sem.at[2 * i], recv_sem=pair_sem.at[2 * i + 1],
+            device_id=(model, gx, 1 - gz), device_id_type=MESH,
+        )
+        copy.start()
+        across.append(copy)
     copies = []
-    distant = sorted(range(1, groups), key=lambda j: -min(j, groups - j))
-    for j in distant:
-        target = lax.rem(gx + j, groups)
-        copy = pltpu.make_async_remote_copy(
-            src_ref=mine.at[:, target],
-            dst_ref=got_x.at[gx],
-            send_sem=send_sem.at[j], recv_sem=recv_sem.at[j],
-            device_id=(model, target, gz), device_id_type=MESH,
-        )
-        copy.start()
-        copies.append(copy)
+    for (begin, count), arrival in zip(spans, across):
+        block = pl.ds(begin, count)
+        arrival.wait_recv()
+        mine[:, block] = partial[gz, :, block] + got_z[:, block]
+        offsets = range(max(begin, 1), begin + count)
+        for j in sorted(offsets, key=lambda j: -min(j, groups - j)):
+            copy = pltpu.make_async_remote_copy(
+                src_ref=mine.at[:, j],
+                dst_ref=got_x.at[j],
+                send_sem=send_sem.at[j], recv_sem=recv_sem.at[j],
+                device_id=(model, lax.rem(gx + j, groups), gz), device_id_type=MESH,
+            )
+            copy.start()
+            copies.append((j, copy))
+
     def third(z, carry):
         values = inner_velocity(z, middle, eta, density, inverse)
         for f in range(3):
@@ -637,50 +643,25 @@
             result[f, :, row] = values[f]
     all_sent([x_u, x_p, x_eta, x_rest, x_u2, x_rest2])
 
-    slot = gz * groups + gx
-    index_x = lax.broadcasted_iota(jnp.int32, (16, total_x), 1)
-    index_y = lax.broadcasted_iota(jnp.int32, (16, total_x), 0) + 16 * slot
-    wx, wy = wave_of(index_x, total_x), wave_of(index_y, NY)
-    scale = gravity_scale * layer_depth / (total_x * NY)
-    weight = scale * jnp.exp((-0.5 * layer_depth) * jnp.sqrt(wx * wx + wy * wy))
-    weight = weight * jnp.where(index_y == 0, jnp.where(index_x == 0, 0.0, 1.0), 2.0)
-    weight = jnp.concatenate([weight, weight], axis=1)
-    summed = mine[:, gx]
-    for j, copy in zip(distant, copies):
+    summed = mine[:, 0]
+    for j, copy in copies:
         copy.wait_recv()
-        summed = summed + got_x[lax.rem(gx + groups - j, groups)]
-    high, low = split_value(summed.reshape(16, 2 * total_x) * weight)
-    both = dot(jnp.concatenate([high, low], axis=0), bx[0])
-    columns = both[:16] + both[16:] + dot(high, bx[1])
-
-    lane = lax.broadcasted_iota(jnp.int32, (8, 128), 1)
-    span = 2 * width
-    for target in range(groups):
-        place = span * target
-        group, offset = place // 128 * 128, place % 128
-        upper = pltpu.roll(columns[:8, group : group + 128], (128 - offset) % 128, 1)
-        lower = pltpu.roll(columns[8:, group : group + 128], (128 + span - offset) % 128, 1)
-        back[target] = jnp.where(lane < span, upper, lower)
-    returns = []
-    for j in sorted(range(1, ranks), key=lambda j: -min(j, ranks - j)):
-        other = lax.rem(rank + j, ranks)
-        copy = pltpu.make_async_remote_copy(
-            src_ref=back.at[other // layers],
-            dst_ref=got_back.at[slot],
-            send_sem=send_sem2.at[j], recv_sem=recv_sem2.at[j],
-            device_id=(model, other // layers, lax.rem(other, layers)), device_id_type=MESH,
-        )
-        copy.start()
-        returns.append(copy)
-    got_back[slot] = back[gx]
-    for copy in returns:
-        copy.wait_recv()
-    waves = jnp.transpose(got_back[...].reshape(8 * ranks, 128))
+        summed = summed + got_x[j]
+    whole[gz] = summed
+    last_copy = pltpu.make_async_remote_copy(
+        src_ref=whole.at[gz], dst_ref=whole.at[gz],
+        send_sem=pair_sem.at[6], recv_sem=pair_sem.at[7],
+        device_id=(model, gx, 1 - gz), device_id_type=MESH,
+    )
+    last_copy.start()
+    for j, copy in copies:
+        copy.wait_send()
+    for copy in across:
+        copy.wait_send()
+    last_copy.wait()
     waves_out[...] = jnp.concatenate(
-        [waves[i * width : (i + 1) * width] for i in (0, 2, 1, 3)], axis=1
-    )
-    for copy in copies + returns:
-        copy.wait_send()
+        [whole[i, part] for i in range(layers) for part in range(2)], axis=1
+    )
 
 
 def last_kernel(result, waves, ty, velocity_out, pressure_out, gravity, sem):
@@ -702,8 +683,9 @@
     depth, width, lateral = pressure.shape
     groups, layers = lax.axis_size("gx"), lax.axis_size("gz")
     total_x = groups * width
-    ty, along_x, phase, bx = host_tables(groups, layers, width, total_x)
-    ranks = groups * layers
+    ty, along_x, bx = host_tables(layers, width, total_x)
+    held = HALF_MODES // layers
+    shares = pltpu.VMEM((2, groups, width, held), jnp.float32)
     f32, b16 = jnp.float32, jnp.bfloat16
     vmem = pl.BlockSpec(memory_space=pltpu.VMEM)
     smem = pl.BlockSpec(memory_space=pltpu.SMEM)
@@ -720,7 +702,7 @@
             pltpu.VMEM((4,) + cells, f32),
             pltpu.VMEM((width, 2 * HALF_MODES), f32),
         ),
-        in_specs=[smem, smem] + [hbm] * 7,
+        in_specs=[smem, smem] + [hbm] * 6,
         out_specs=(vmem, vmem),
         scratch_shapes=[
             pltpu.VMEM(cells, jnp.int32),
@@ -733,24 +715,21 @@
             eta_rows, eta_rows, eta_rows, eta_rows,
             pltpu.VMEM(ty.shape, b16),
             pltpu.VMEM(along_x.shape, b16),
-            pltpu.VMEM(phase.shape, f32),
             pltpu.VMEM(bx.shape, b16),
             pltpu.VMEM(cells, f32),
-            pltpu.VMEM((2, ranks, 8, 2 * total_x), f32),
-            pltpu.VMEM((2, groups, 8, 2 * total_x), f32),
-            pltpu.VMEM((2, groups, 8, 2 * total_x), f32),
-            pltpu.VMEM((groups, 2, 8, 2 * total_x), f32),
-            pltpu.VMEM((groups, 8, 128), f32),
-            pltpu.VMEM((ranks, 8, 128), f32),
-            sems((7,)), sems((6,)), sems((24,)), sems((2,)),
-            sems((groups,)), sems((groups,)), sems((ranks,)), sems((ranks,)),
+            pltpu.VMEM((layers, 2, groups, width, held), f32),
+            shares, shares,
+            pltpu.VMEM((groups, 2, width, held), f32),
+            pltpu.VMEM((layers, 2, width, held), f32),
+            sems((6,)), sems((6,)), sems((24,)), sems((8,)),
+            sems((groups,)), sems((groups,)),
         ],
         compiler_params=pltpu.CompilerParams(
             collective_id=0, has_side_effects=True, vmem_limit_bytes=56 * 1024 * 1024
         ),
     )(
         density_table, viscosity_table, phases, velocity, pressure,
-        along_y, jnp.asarray(along_x), jnp.asarray(phase), jnp.asarray(bx),
+        along_y, jnp.asarray(along_x), jnp.asarray(bx),
     )
     return pl.pallas_call(
         last_kernel,

time: 31 us -> 25.2 us (0.81)
  Pallas kernels: 30.2 us -> 24.3 us
    pallas_call x1, Pallas kernels: 28.5 us -> 22.7 us  [fused_body(): pl.pallas_call(functools.partial(kernel, groups, layers), out_shape=(pltp...]
where the time goes in v3:
time: 25.2 us; the launch traced here: 25 us
  Pallas kernels  24.3 us (96%)
  between operations  0.66 us (3%)
    pallas_call x1, Pallas kernels, fused_body(): pl.pallas_call(functools.partial(kernel, groups, layers), out_shape=(pltp...  22.7 us
    pallas_call x1, Pallas kernels, fused_body(): pl.pallas_call(last_kernel, out_shape=(jax.ShapeDtypeStruct(velocity.shap...  1.66 us

profile of v3, /device:TPU:0, one launch (start us, length us, event | category | flops | bytes accessed | tf_op | source)
XLA Modules:
  0.0 25.0 jit_solution(33020899965054938)
XLA Ops:
  0.6 0.0 copy-start
  0.6 22.7 %shard_map.103 = (f32[4,8,16,512]{3,2,1,0:T(8,128)S(1)}, f32[16,512]{1,0:T(8,128)S(1)}) custom-call(f32[8]{0:T(128)} %dens_ref.1, f32[8]{0:T(128)} %visc_ref.1, s32[8,16,512]{2,1,0:T(8,128)} %phases_hbm.1, f32[3,8,16,512]{3,2,1,0:T(8,128)} %velocity_hbm.1, f32[8,16,512]{2,1,0:T(8,128)} %pressure_hbm.1, bf16[2,512,512]{2,1,0:T(8,128)(2,1)} %constant.6.clone.ty_hbm.ty, ...), custom_call_target="tpu_custom_call" | custom-call | tf_op jit(solution)/shard_map/pallas_call | solution.py:699
  23.3 0.0 copy-done
  23.3 1.7 %shard_map.104 = (f32[3,8,16,512]{3,2,1,0:T(8,128)}, f32[8,16,512]{2,1,0:T(8,128)}, f32[16,512]{1,0:T(8,128)}) custom-call(f32[4,8,16,512]{3,2,1,0:T(8,128)S(1)} %get-tuple-element.5.result, f32[16,512]{1,0:T(8,128)S(1)} %get-tuple-element.6.waves, bf16[2,512,512]{2,1,0:T(8,128)(2,1)S(1)} %copy-done), custom_call_target="tpu_custom_call" | custom-call | tf_op jit(solution)/shard_map/pallas_call | solution.py:734
Async XLA Ops:
  0.6 22.7 %copy-start = (bf16[2,512,512]{2,1,0:T(8,128)(2,1)S(1)}, bf16[2,512,512]{2,1,0:T(8,128)(2,1)}, u32[]{:S(2)}) copy-start(bf16[2,512,512]{2,1,0:T(8,128)(2,1)} %constant.6.clone.ty_hbm.ty) | copy-start | bytes 3145732

commit v4 on v3

--- a/solution.py
+++ b/solution.py
@@ -374,8 +374,6 @@
     model, gx, gz = lax.axis_index("models"), lax.axis_index("gx"), lax.axis_index("gz")
     depth, width, lateral = density.shape
     total_x = groups * width
-    ranks = groups * layers
-    rank = gx * layers + gz
     last = width - 1
 
     loads = [
@@ -395,11 +393,10 @@
         copy.start()
 
     barrier = pltpu.get_barrier_semaphore()
-    for j in range(1, ranks):
-        other = lax.rem(rank + j, ranks)
+    partners = [(lax.rem(gx + j, groups), gz) for j in range(1, groups)] + [(gx, 1 - gz)]
+    for other_x, other_z in partners:
         pl.semaphore_signal(
-            barrier, inc=1, device_id=(model, other // layers, lax.rem(other, layers)),
-            device_id_type=MESH,
+            barrier, inc=1, device_id=(model, other_x, other_z), device_id_type=MESH
         )
 
     edge = (depth + 1) * gz
@@ -496,7 +493,7 @@
     for f in range(4):
         send_low[f] = fields[f, 1 : depth + 1, 0]
         send_high[f] = fields[f, 1 : depth + 1, last]
-    pl.semaphore_wait(barrier, ranks - 1)
+    pl.semaphore_wait(barrier, len(partners))
     send([x_u, x_p])
     z_first = beside_z(0, fields.at[:, facing], fields.at[:, edge])
 
@@ -689,7 +686,6 @@
     f32, b16 = jnp.float32, jnp.bfloat16
     vmem = pl.BlockSpec(memory_space=pltpu.VMEM)
     smem = pl.BlockSpec(memory_space=pltpu.SMEM)
-    anywhere = pl.BlockSpec(memory_space=pl.ANY)
     hbm = pl.BlockSpec(memory_space=pltpu.HBM)
     rows = pltpu.VMEM((4, depth, lateral), f32)
     eta_rows = pltpu.VMEM((depth, lateral), f32)

time: 25.2 us -> 24.7 us (0.980)
  Pallas kernels: 24.3 us -> 23.9 us
    pallas_call x1, Pallas kernels: 22.7 us -> 22.2 us  [fused_body(): pl.pallas_call(functools.partial(kernel, groups, layers), out_shape=(pltp...]
where the time goes in v4:
time: 24.7 us; the launch traced here: 24.5 us
  Pallas kernels  23.9 us (97%)
  between operations  0.66 us (3%)
    pallas_call x1, Pallas kernels, fused_body(): pl.pallas_call(functools.partial(kernel, groups, layers), out_shape=(pltp...  22.2 us
    pallas_call x1, Pallas kernels, fused_body(): pl.pallas_call(last_kernel, out_shape=(jax.ShapeDtypeStruct(velocity.shap...  1.66 us

profile of v4, /device:TPU:0, one launch (start us, length us, event | category | flops | bytes accessed | tf_op | source)
XLA Modules:
  0.0 24.5 jit_solution(12155893967428296882)
XLA Ops:
  0.6 0.0 copy-start
  0.6 22.2 %shard_map.103 = (f32[4,8,16,512]{3,2,1,0:T(8,128)S(1)}, f32[16,512]{1,0:T(8,128)S(1)}) custom-call(f32[8]{0:T(128)} %dens_ref.1, f32[8]{0:T(128)} %visc_ref.1, s32[8,16,512]{2,1,0:T(8,128)} %phases_hbm.1, f32[3,8,16,512]{3,2,1,0:T(8,128)} %velocity_hbm.1, f32[8,16,512]{2,1,0:T(8,128)} %pressure_hbm.1, bf16[2,512,512]{2,1,0:T(8,128)(2,1)} %constant.6.clone.ty_hbm.ty, ...), custom_call_target="tpu_custom_call" | custom-call | tf_op jit(solution)/shard_map/pallas_call | solution.py:695
  22.8 0.0 copy-done
  22.9 1.7 %shard_map.104 = (f32[3,8,16,512]{3,2,1,0:T(8,128)}, f32[8,16,512]{2,1,0:T(8,128)}, f32[16,512]{1,0:T(8,128)}) custom-call(f32[4,8,16,512]{3,2,1,0:T(8,128)S(1)} %get-tuple-element.5.result, f32[16,512]{1,0:T(8,128)S(1)} %get-tuple-element.6.waves, bf16[2,512,512]{2,1,0:T(8,128)(2,1)S(1)} %copy-done), custom_call_target="tpu_custom_call" | custom-call | tf_op jit(solution)/shard_map/pallas_call | solution.py:730
Async XLA Ops:
  0.6 22.2 %copy-start = (bf16[2,512,512]{2,1,0:T(8,128)(2,1)S(1)}, bf16[2,512,512]{2,1,0:T(8,128)(2,1)}, u32[]{:S(2)}) copy-start(bf16[2,512,512]{2,1,0:T(8,128)(2,1)} %constant.6.clone.ty_hbm.ty) | copy-start | bytes 3145732

commit v5 on v4

--- a/solution.py
+++ b/solution.py
@@ -568,15 +568,24 @@
     weight = weight * jnp.where(index_y == 0, jnp.where(index_x == 0, 0.0, 1.0), 2.0)
     for copy in loads[3:]:
         copy.wait()
+    def along_y(value):
+        count = value.shape[0]
+        high, low = split_value(value)
+        both = dot(jnp.concatenate([high, low], axis=0), ty[0])
+        return both[:count] + both[count:] + dot(high, ty[1])
+
+    loaded[...] = along_y(loaded[...].reshape(depth * width, lateral)).reshape(loaded.shape)
+    edge_loads = []
     for row, halo, eta_halo, out, later in edges:
         receive([x_u2], row)
         pressure = edge_pressure(row, middle, later, fields)
         result[3, :, row] = pressure
-        loaded[:, row] = density[:, row] * (1.0 + squeeze * pressure)
-
-    high, low = split_value(loaded[...].reshape(depth * width, lateral))
-    both = dot(jnp.concatenate([high, low], axis=0), ty[0])
-    rows = both[: depth * width] + both[depth * width :] + dot(high, ty[1])
+        edge_loads.append(density[:, row] * (1.0 + squeeze * pressure))
+    edge_modes = along_y(jnp.concatenate(edge_loads, axis=0))
+    loaded[:, 0] = edge_modes[:depth]
+    loaded[:, last] = edge_modes[depth:]
+
+    rows = loaded[...].reshape(depth * width, 2 * HALF_MODES)
     held = HALF_MODES // layers
     parts = [rows[:, held * i : held * (i + 1)] for i in range(2 * layers)]
     real = jnp.concatenate(parts[0::2], axis=1)

time: 24.7 us -> 24.6 us (level)
  no operation moved by 1% of the time
where the time goes in v5:
time: 24.6 us; the launch traced here: 24.4 us
  Pallas kernels  23.8 us (97%)
  between operations  0.66 us (3%)
    pallas_call x1, Pallas kernels, fused_body(): pl.pallas_call(functools.partial(kernel, groups, layers), out_shape=(pltp...  22.1 us
    pallas_call x1, Pallas kernels, fused_body(): pl.pallas_call(last_kernel, out_shape=(jax.ShapeDtypeStruct(velocity.shap...  1.66 us

profile of v5, /device:TPU:0, one launch (start us, length us, event | category | flops | bytes accessed | tf_op | source)
XLA Modules:
  0.0 24.4 jit_solution(16663489922398389489)
XLA Ops:
  0.6 0.0 copy-start
  0.6 22.1 %shard_map.103 = (f32[4,8,16,512]{3,2,1,0:T(8,128)S(1)}, f32[16,512]{1,0:T(8,128)S(1)}) custom-call(f32[8]{0:T(128)} %dens_ref.1, f32[8]{0:T(128)} %visc_ref.1, s32[8,16,512]{2,1,0:T(8,128)} %phases_hbm.1, f32[3,8,16,512]{3,2,1,0:T(8,128)} %velocity_hbm.1, f32[8,16,512]{2,1,0:T(8,128)} %pressure_hbm.1, bf16[2,512,512]{2,1,0:T(8,128)(2,1)} %constant.6.clone.ty_hbm.ty, ...), custom_call_target="tpu_custom_call" | custom-call | tf_op jit(solution)/shard_map/pallas_call | solution.py:704
  22.7 0.0 copy-done
  22.8 1.7 %shard_map.104 = (f32[3,8,16,512]{3,2,1,0:T(8,128)}, f32[8,16,512]{2,1,0:T(8,128)}, f32[16,512]{1,0:T(8,128)}) custom-call(f32[4,8,16,512]{3,2,1,0:T(8,128)S(1)} %get-tuple-element.5.result, f32[16,512]{1,0:T(8,128)S(1)} %get-tuple-element.6.waves, bf16[2,512,512]{2,1,0:T(8,128)(2,1)S(1)} %copy-done), custom_call_target="tpu_custom_call" | custom-call | tf_op jit(solution)/shard_map/pallas_call | solution.py:739
Async XLA Ops:
  0.6 22.1 %copy-start = (bf16[2,512,512]{2,1,0:T(8,128)(2,1)S(1)}, bf16[2,512,512]{2,1,0:T(8,128)(2,1)}, u32[]{:S(2)}) copy-start(bf16[2,512,512]{2,1,0:T(8,128)(2,1)} %constant.6.clone.ty_hbm.ty) | copy-start | bytes 3145732
